TPU v7x, 128 devices: a whole 4x4x4 slice. The times are simulated.
128 devices in a mesh: pb: 32 (over x, y, core), pa: 4 (over z).
Axes of the slice: x: 4, y: 4, z: 4, core: 2. Of those that a mesh axis runs over, the one named last changes fastest.
Arguments:
- queries: bfloat16 [4096, 4096], P(('pb', 'pa')), may hold values from -4 to 4
- passages: bfloat16 [16384, 4096], P(('pb', 'pa')), may hold values from -4 to 4
- query_cluster: int32 [4096], P(('pb', 'pa')), may hold values from 0 to 255, as said below
- passage_cluster: int32 [16384], P(('pb', 'pa')), may hold values from 0 to 511, as said below
- allowed: int32 [256, 16], replicated, may hold values from 0 to 1, as said below
- positive: int32 [4096], P(('pb', 'pa')), may hold values from 0 to 16383, as said below
Outputs:
- grad_queries: bfloat16 [4096, 4096], P(('pb', 'pa'))
- grad_passages: bfloat16 [16384, 4096], P(('pb', 'pa'))
Inputs may be any that keep to these rules, and one draw needn't show every extreme that they name: `query_cluster`: on each device's rows, at most 2 queries have a cluster in any one block of 8 consecutive clusters, and some block has exactly 2. `passage_cluster`: on each device's rows, at most 2 passages have a cluster in any one block of 4 consecutive clusters, and some block has exactly 2. allowed[query_cluster[i], passage_cluster[positive[i]] - (query_cluster[i] // 8) * 16] == 1 for every query i. passage_cluster[positive[i]] // 16 == query_cluster[i] // 8 for every query i.
All inputs are finite; a program needn't handle non-finite values.
Results may differ from a plain program's by a relative error of at most 0.012.
Values may be sent and summed in bfloat16 or wider, within the bound.
A program may use at most 64 MiB of HBM per device.

v0:
```python
import jax
import jax.numpy as jnp
from jax import lax
from jax.sharding import PartitionSpec as P

QCL = 8
PCL = 4


inv_temp = 50.0
neg_fill = -1e30


def slot_index(targets, num_targets, capacity):
    one_hot = (targets[:, None] == jnp.arange(num_targets, dtype=jnp.int32)[None, :]).astype(
        jnp.int32
    )
    before = jnp.sum((jnp.cumsum(one_hot, axis=0) - one_hot) * one_hot, axis=1)
    return targets * capacity + before


def per_device(queries, passages, query_cluster, passage_cluster, allowed, positive):
    n_rows = lax.axis_size("pb")
    n_cols = lax.axis_size("pa")
    devices = n_rows * n_cols
    q_local = queries.shape[0]
    emb_width = queries.shape[1]
    p_local = passages.shape[0]
    q_cap = 2 * q_local // n_rows
    p_cap = 2 * p_local // devices
    row_index = lax.axis_index("pb")
    col_index = lax.axis_index("pa")
    owner_id = row_index * n_cols + col_index
    block_span = PCL * n_cols
    q_slot = slot_index(query_cluster // QCL, n_rows, q_cap)
    sent_q = jnp.zeros((n_rows * q_cap, emb_width), jnp.bfloat16).at[q_slot].set(queries)
    sent_qcl = jnp.full((n_rows * q_cap,), -1, jnp.int32).at[q_slot].set(query_cluster)
    sent_pos = jnp.full((n_rows * q_cap,), -1, jnp.int32).at[q_slot].set(positive)
    got_q, got_qcl, got_pos = (
        lax.all_to_all(
            sent_q.reshape(n_rows, q_cap, emb_width), "pb", split_axis=0, concat_axis=0, tiled=True
        ),
        lax.all_to_all(
            sent_qcl.reshape(n_rows, q_cap), "pb", split_axis=0, concat_axis=0, tiled=True
        ),
        lax.all_to_all(
            sent_pos.reshape(n_rows, q_cap), "pb", split_axis=0, concat_axis=0, tiled=True
        ),
    )
    owner_q, owner_qcl, owner_pos = (
        lax.all_gather(got_q.reshape(n_rows * q_cap, emb_width), "pa", axis=0, tiled=True),
        lax.all_gather(got_qcl.reshape(n_rows * q_cap), "pa", axis=0, tiled=True),
        lax.all_gather(got_pos.reshape(n_rows * q_cap), "pa", axis=0, tiled=True),
    )
    p_slot = slot_index(passage_cluster // PCL, devices, p_cap)
    passage_number = owner_id * p_local + jnp.arange(p_local, dtype=jnp.int32)
    sent_p = jnp.zeros((devices * p_cap, emb_width), jnp.bfloat16).at[p_slot].set(passages)
    sent_pcl = jnp.full((devices * p_cap,), -1, jnp.int32).at[p_slot].set(passage_cluster)
    sent_pid = jnp.full((devices * p_cap,), -1, jnp.int32).at[p_slot].set(passage_number)
    got_p, got_pcl, got_pid = (
        lax.all_to_all(
            sent_p.reshape(devices, p_cap, emb_width),
            ("pb", "pa"),
            split_axis=0,
            concat_axis=0,
            tiled=True,
        ),
        lax.all_to_all(
            sent_pcl.reshape(devices, p_cap), ("pb", "pa"), split_axis=0, concat_axis=0, tiled=True
        ),
        lax.all_to_all(
            sent_pid.reshape(devices, p_cap), ("pb", "pa"), split_axis=0, concat_axis=0, tiled=True
        ),
    )
    owner_p = got_p.reshape(devices * p_cap, emb_width)
    owner_pcl = got_pcl.reshape(devices * p_cap)
    owner_pid = got_pid.reshape(devices * p_cap)
    query_live = owner_qcl >= 0
    query_local = jnp.where(query_live, owner_qcl % QCL, -1)
    wanted = jnp.where(query_live, owner_pos, -2)
    passage_live = owner_pid >= 0
    passage_local = jnp.where(passage_live, owner_pcl - row_index * block_span, -1)
    pair_table = lax.dynamic_slice_in_dim(allowed, row_index * QCL, QCL, 0).astype(jnp.float32)
    query_onehot = (query_local[:, None] == jnp.arange(QCL, dtype=jnp.int32)[None, :]).astype(
        jnp.float32
    )
    passage_onehot = (
        passage_local[:, None] == jnp.arange(block_span, dtype=jnp.int32)[None, :]
    ).astype(jnp.float32)
    reach = jnp.dot(query_onehot, pair_table, precision=lax.Precision.HIGHEST)
    permitted = (
        lax.dot_general(
            reach, passage_onehot, (((1,), (1,)), ((), ())), precision=lax.Precision.HIGHEST
        )
        > 0.5
    )
    targets = ((wanted[:, None] == owner_pid[None, :]) & passage_live[None, :]).astype(jnp.float32)
    scores = (
        lax.dot_general(
            owner_q, owner_p, (((1,), (1,)), ((), ())), preferred_element_type=jnp.float32
        )
        * inv_temp
    )
    local_top = jnp.max(jnp.where(permitted, scores, neg_fill), axis=1)
    row_top = lax.pmax(local_top, "pa")
    exp_terms = jnp.where(permitted, jnp.exp(scores - row_top[:, None]), 0.0)
    row_total = lax.psum(jnp.sum(exp_terms, axis=1), "pa")
    softmax_p = exp_terms / jnp.where(row_total > 0.0, row_total, 1.0)[:, None]
    grad_scores = ((softmax_p - targets) * inv_temp).astype(jnp.bfloat16)
    query_part = jnp.dot(grad_scores, owner_p, preferred_element_type=jnp.float32)
    passage_grad = lax.dot_general(
        grad_scores, owner_q, (((0,), (0,)), ((), ())), preferred_element_type=jnp.float32
    ).astype(jnp.bfloat16)
    query_sum = lax.psum_scatter(
        query_part.astype(jnp.bfloat16), "pa", scatter_dimension=0, tiled=True
    )
    back_q = lax.all_to_all(
        query_sum.reshape(n_rows, q_cap, emb_width), "pb", split_axis=0, concat_axis=0, tiled=True
    )
    grad_queries = back_q.reshape(n_rows * q_cap, emb_width)[q_slot]
    back_p = lax.all_to_all(
        passage_grad.reshape(devices, p_cap, emb_width),
        ("pb", "pa"),
        split_axis=0,
        concat_axis=0,
        tiled=True,
    )
    grad_passages = back_p.reshape(devices * p_cap, emb_width)[p_slot]
    return (grad_queries, grad_passages)


def solution(mesh):
    in_specs = (
        P(("pb", "pa"), None),
        P(("pb", "pa"), None),
        P(("pb", "pa")),
        P(("pb", "pa")),
        P(),
        P(("pb", "pa")),
    )
    out_specs = (P(("pb", "pa"), None), P(("pb", "pa"), None))
    return jax.shard_map(
        per_device, mesh=mesh, in_specs=in_specs, out_specs=out_specs, check_vma=False
    )
```

profile of v0, /device:TPU:1, one launch (start us, length us, event | category | flops | bytes accessed | tf_op | source)
XLA Modules:
  0.0 229.1 jit_solution(967063314454359523)
XLA Ops:
  7.2 0.7 and_select_fusion.2
  8.2 0.7 compare_select_fusion.2
  8.9 1.6 scatter_custom_fusion.3
  10.4 0.3 reshape.87
  10.8 20.0 %all_to_all.56 = bf16[32,2,4096]{2,1,0:T(2,128)(2,1)S(1)} all-to-all(bf16[32,2,4096]{2,1,0:T(2,128)(2,1)S(1)} %reshape.87), channel_id=1, replica_groups=mesh['pb'=32,'pa'=4] {'pb'}, dimensions={0} | all-to-all | bytes 1048576 | tf_op jit(solution)/shard_map/all_to_all | solution.py:40
  30.8 1.0 reshape.88
  31.8 0.8 scatter_custom_fusion
  32.6 0.7 all_to_all.36
  33.3 3.6 %all-to-all-start = ((s32[32,1,2]{2,1,0:T(1,128)}), s32[32,1,2]{2,1,0:T(1,128)S(1)}, u32[]{:S(2)}, u32[]{:S(2)}) async-start(s32[32,1,2]{2,1,0:T(1,128)} %bitcast), calls=%async_computation | async-start | bytes 32768 | tf_op jit(solution)/shard_map/all_to_all | solution.py:43
  37.0 0.8 scatter_custom_fusion.5
  37.8 0.7 all_to_all.44
  38.9 4.9 %all-to-all-done = s32[32,1,2]{2,1,0:T(1,128)S(1)} async-done(((s32[32,1,2]{2,1,0:T(1,128)}), s32[32,1,2]{2,1,0:T(1,128)S(1)}, u32[]{:S(2)}, u32[]{:S(2)}) %all-to-all-start) | async-done | bytes 288 | tf_op jit(solution)/shard_map/all_to_all | solution.py:43
  43.8 4.1 %all-to-all-start.5 = ((s32[32,1,2]{2,1,0:T(1,128)}), s32[32,1,2]{2,1,0:T(1,128)S(1)}, u32[]{:S(2)}, u32[]{:S(2)}) async-start(s32[32,1,2]{2,1,0:T(1,128)} %bitcast.4), calls=%async_computation.5 | async-start | bytes 32768 | tf_op jit(solution)/shard_map/all_to_all | solution.py:46
  47.9 1.0 scatter_custom_fusion.2
  48.9 0.8 all_to_all.40
  49.7 5.3 %all-to-all-done.5 = s32[32,1,2]{2,1,0:T(1,128)S(1)} async-done(((s32[32,1,2]{2,1,0:T(1,128)}), s32[32,1,2]{2,1,0:T(1,128)S(1)}, u32[]{:S(2)}, u32[]{:S(2)}) %all-to-all-start.5) | async-done | bytes 288 | tf_op jit(solution)/shard_map/all_to_all | solution.py:46
  55.0 6.8 %all-to-all-start.2 = ((s32[128,1,2]{2,1,0:T(1,128)}), s32[128,1,2]{2,1,0:T(1,128)S(1)}, u32[]{:S(2)}, u32[]{:S(2)}) async-start(s32[128,1,2]{2,1,0:T(1,128)} %bitcast.3), calls=%async_computation.2 | async-start | bytes 131072 | tf_op jit(solution)/shard_map/all_to_all | solution.py:68
  61.8 1.0 scatter_custom_fusion.1
  62.8 0.8 all_to_all.38
  63.6 7.9 %all-to-all-done.2 = s32[128,1,2]{2,1,0:T(1,128)S(1)} async-done(((s32[128,1,2]{2,1,0:T(1,128)}), s32[128,1,2]{2,1,0:T(1,128)S(1)}, u32[]{:S(2)}, u32[]{:S(2)}) %all-to-all-start.2) | async-done | bytes 1056 | tf_op jit(solution)/shard_map/all_to_all | solution.py:68
  71.4 4.3 %all-to-all-start.1 = ((s32[128,1,2]{2,1,0:T(1,128)}), s32[128,1,2]{2,1,0:T(1,128)S(1)}, u32[]{:S(2)}, u32[]{:S(2)}) async-start(s32[128,1,2]{2,1,0:T(1,128)} %bitcast.2), calls=%async_computation.1 | async-start | bytes 131072 | tf_op jit(solution)/shard_map/all_to_all | solution.py:71
  75.7 3.4 %scatter_custom_fusion.4 = bf16[256,4096]{1,0:T(8,128)(2,1)S(1)} fusion(s32[128]{0:T(128)S(1)} %get-tuple-element.10, bf16[128,4096]{1,0:T(8,128)(2,1)} %param.7, bf16[]{:T(256)} %constant.87.clone.1), kind=kCustom, calls=%fused_computation.12 | custom fusion | bytes 2097664 | tf_op jit(solution)/shard_map/scatter | solution.py:57
  79.1 2.7 %reshape.89 = bf16[128,2,4096]{2,1,0:T(2,128)(2,1)} reshape(bf16[256,4096]{1,0:T(8,128)(2,1)S(1)} %scatter_custom_fusion.4) | data formatting | bytes 4194304 | tf_op jit(solution)/shard_map/reshape | solution.py:62
  81.8 3.6 %all-to-all-done.1 = s32[128,1,2]{2,1,0:T(1,128)S(1)} async-done(((s32[128,1,2]{2,1,0:T(1,128)}), s32[128,1,2]{2,1,0:T(1,128)S(1)}, u32[]{:S(2)}, u32[]{:S(2)}) %all-to-all-start.1) | async-done | bytes 1056 | tf_op jit(solution)/shard_map/all_to_all | solution.py:71
  85.4 6.6 %all-to-all-start.4 = ((bf16[128,2,4096]{2,1,0:T(2,128)(2,1)}), bf16[128,2,4096]{2,1,0:T(2,128)(2,1)}, u32[]{:S(2)}, u32[]{:S(2)}) async-start(bf16[128,2,4096]{2,1,0:T(2,128)(2,1)} %reshape.89), calls=%async_computation.4 | async-start | bytes 4194304 | tf_op jit(solution)/shard_map/all_to_all | solution.py:61
  92.1 0.6 dynamic-slice
  93.3 0.5 broadcast.120
  93.8 0.7 reduce.13
  94.6 0.7 reduce.15
  95.9 10.7 %all-reduce.2 = (s32[256]{0:T(256)S(1)}, s32[256]{0:T(256)S(1)}) all-reduce(s32[256]{0:T(256)S(1)} %dynamic-update-slice, s32[256]{0:T(256)S(1)} %dynamic-update-slice.1), channel_id=1, replica_groups=mesh['pb'=32,'pa'=4] {'pa'}, use_global_device_ids=true, to_apply=%add | all-reduce | flops 512 | bytes 4096
  107.2 0.8 reduce.14
  108.2 14.3 %all-to-all-done.4 = bf16[128,2,4096]{2,1,0:T(2,128)(2,1)} async-done(((bf16[128,2,4096]{2,1,0:T(2,128)(2,1)}), bf16[128,2,4096]{2,1,0:T(2,128)(2,1)}, u32[]{:S(2)}, u32[]{:S(2)}) %all-to-all-start.4) | async-done | bytes 2097184 | tf_op jit(solution)/shard_map/all_to_all | solution.py:61
  122.5 2.7 %reshape.90 = bf16[256,4096]{1,0:T(8,128)(2,1)S(1)} reshape(bf16[128,2,4096]{2,1,0:T(2,128)(2,1)} %all-to-all-done.4) | data formatting | bytes 4194304 | tf_op jit(solution)/shard_map/reshape | solution.py:75
  125.3 2.3 %convolution_multiply_fusion = f32[256,256]{0,1:T(8,128)S(1)} fusion(bf16[256,4096]{1,0:T(8,128)(2,1)} %all-gather.2.cloned.1.call-done, bf16[256,4096]{1,0:T(8,128)(2,1)S(1)} %reshape.90), kind=kOutput, calls=%fused_computation.10 | convolution fusion | flops 536936448 | bytes 4456448 | tf_op jit(solution)/shard_map/dot_general | solution.py:99
  127.6 0.3 select_reduce_fusion
  127.9 6.5 %pmax.7 = f32[256]{0:T(256)S(1)} all-reduce(f32[256]{0:T(256)S(1)} %get-tuple-element.8), channel_id=1, replica_groups=mesh['pb'=32,'pa'=4] {'pa'}, use_global_device_ids=true, to_apply=%region_10.11 | all-reduce | flops 256 | bytes 2048 | tf_op jit(solution)/shard_map/pmax | solution.py:105
  134.6 6.9 %psum.7 = f32[256]{0:T(256)S(1)} all-reduce(f32[256]{0:T(256)S(1)} %fusion.4), channel_id=1, replica_groups=mesh['pb'=32,'pa'=4] {'pa'}, use_global_device_ids=true, to_apply=%region_12.13 | all-reduce | flops 256 | bytes 2048 | tf_op jit(solution)/shard_map/psum | solution.py:107
  141.5 2.2 convolution_convert_fusion.1
  143.7 2.4 %convolution_convert_fusion = bf16[256,4096]{1,0:T(8,128)(2,1)S(1)} fusion(bf16[256,4096]{1,0:T(8,128)(2,1)} %all-gather.2.cloned.1.call-done, pred[256,256]{0,1:T(32,128)(4,1)S(1)} %get-tuple-element.9, f32[256,256]{0,1:T(8,128)S(1)} %convolution_multiply_fusion, s32[256]{0:T(256)S(1)} %get-tuple-element.6, f32[256]{0:T(256)S(1)} %compare_select_fusion, ...), kind=kOutput, calls=%fused_computation.8 | convolution fusion | flops 538509312 | bytes 4526336 | tf_op jit(solution)/shard_map/dot_general | solution.py:111
  146.0 2.7 %reshape.94 = bf16[128,2,4096]{2,1,0:T(2,128)(2,1)} reshape(bf16[256,4096]{1,0:T(8,128)(2,1)S(1)} %convolution_convert_fusion) | data formatting | bytes 4194304 | tf_op jit(solution)/shard_map/reshape | solution.py:122
  148.7 11.4 %all-to-all-start.7 = ((bf16[128,2,4096]{2,1,0:T(2,128)(2,1)}), bf16[128,2,4096]{2,1,0:T(2,128)(2,1)S(1)}, u32[]{:S(2)}, u32[]{:S(2)}) async-start(bf16[128,2,4096]{2,1,0:T(2,128)(2,1)} %reshape.94), calls=%async_computation.8 | async-start | bytes 4194304 | tf_op jit(solution)/shard_map/all_to_all | solution.py:121
  160.1 39.2 %reduce-scatter.2.cloned.1.call-done = bf16[64,4096]{1,0:T(8,128)(2,1)} async-done(((bf16[256,4096]{1,0:T(8,128)(2,1)}), bf16[64,4096]{1,0:T(8,128)(2,1)}) %reduce-scatter.2.cloned.1.call-update) | async-done | bytes 524304 | tf_op jit(solution)/shard_map/reduce_scatter | solution.py:114
  199.3 2.2 reshape.92
  201.5 7.5 %all-to-all-start.6 = ((bf16[32,2,4096]{2,1,0:T(2,128)(2,1)}), bf16[32,2,4096]{2,1,0:T(2,128)(2,1)S(1)}, u32[]{:S(2)}, u32[]{:S(2)}) async-start(bf16[32,2,4096]{2,1,0:T(2,128)(2,1)} %reshape.92), calls=%async_computation.7 | async-start | bytes 1048576 | tf_op jit(solution)/shard_map/all_to_all | solution.py:117
  209.0 2.7 %reshape.95 = bf16[256,4096]{1,0:T(8,128)(2,1)S(1)} reshape(bf16[128,2,4096]{2,1,0:T(2,128)(2,1)} %copy-done) | data formatting | bytes 4194304 | tf_op jit(solution)/shard_map/reshape | solution.py:128
  211.8 2.2 gather_fusion.1
  214.0 6.7 %all-to-all-done.6 = bf16[32,2,4096]{2,1,0:T(2,128)(2,1)S(1)} async-done(((bf16[32,2,4096]{2,1,0:T(2,128)(2,1)}), bf16[32,2,4096]{2,1,0:T(2,128)(2,1)S(1)}, u32[]{:S(2)}, u32[]{:S(2)}) %all-to-all-start.6) | async-done | bytes 524320 | tf_op jit(solution)/shard_map/all_to_all | solution.py:117
  220.8 1.4 gather_fusion
  (39 shorter events, 2.6 us)
Async XLA Ops:
  7.2 118.1 %all-gather.2.cloned.1.call-start = ((), (), s32[]{:S(2)}) async-start(), calls=%async_computation.9 | async-start | bytes 2621440 | tf_op jit(solution)/shard_map/all_gather | solution.py:51
  8.9 29.6 %copy-start.1 = (s32[128]{0:T(128)S(1)}, s32[128]{0:T(128)}, u32[]{:S(2)}) copy-start(s32[128]{0:T(128)} %param.9) | copy-start | bytes 1540
  33.3 10.5 %all-to-all-start = ((s32[32,1,2]{2,1,0:T(1,128)}), s32[32,1,2]{2,1,0:T(1,128)S(1)}, u32[]{:S(2)}, u32[]{:S(2)}) async-start(s32[32,1,2]{2,1,0:T(1,128)} %bitcast), calls=%async_computation | async-start | bytes 32768 | tf_op jit(solution)/shard_map/all_to_all | solution.py:43
  43.8 11.1 %all-to-all-start.5 = ((s32[32,1,2]{2,1,0:T(1,128)}), s32[32,1,2]{2,1,0:T(1,128)S(1)}, u32[]{:S(2)}, u32[]{:S(2)}) async-start(s32[32,1,2]{2,1,0:T(1,128)} %bitcast.4), calls=%async_computation.5 | async-start | bytes 32768 | tf_op jit(solution)/shard_map/all_to_all | solution.py:46
  55.0 16.5 %all-to-all-start.2 = ((s32[128,1,2]{2,1,0:T(1,128)}), s32[128,1,2]{2,1,0:T(1,128)S(1)}, u32[]{:S(2)}, u32[]{:S(2)}) async-start(s32[128,1,2]{2,1,0:T(1,128)} %bitcast.3), calls=%async_computation.2 | async-start | bytes 131072 | tf_op jit(solution)/shard_map/all_to_all | solution.py:68
  71.4 13.9 %all-to-all-start.1 = ((s32[128,1,2]{2,1,0:T(1,128)}), s32[128,1,2]{2,1,0:T(1,128)S(1)}, u32[]{:S(2)}, u32[]{:S(2)}) async-start(s32[128,1,2]{2,1,0:T(1,128)} %bitcast.2), calls=%async_computation.1 | async-start | bytes 131072 | tf_op jit(solution)/shard_map/all_to_all | solution.py:71
  81.8 10.3 %copy-start.3 = (u32[128]{0:T(128)S(1)}, u32[128]{0:T(128)}, u32[]{:S(2)}) copy-start(u32[128]{0:T(128)} %constant.99) | copy-start | bytes 1540
  81.8 24.9 %copy-start.2 = (s32[256,16]{0,1:T(8,128)S(1)}, s32[256,16]{0,1:T(8,128)}, u32[]{:S(2)}) copy-start(s32[256,16]{0,1:T(8,128)} %param.10) | copy-start | bytes 49156
  85.4 37.1 %all-to-all-start.4 = ((bf16[128,2,4096]{2,1,0:T(2,128)(2,1)}), bf16[128,2,4096]{2,1,0:T(2,128)(2,1)}, u32[]{:S(2)}, u32[]{:S(2)}) async-start(bf16[128,2,4096]{2,1,0:T(2,128)(2,1)} %reshape.89), calls=%async_computation.4 | async-start | bytes 4194304 | tf_op jit(solution)/shard_map/all_to_all | solution.py:61
  92.0 107.3 %reduce-scatter.2.cloned.1.call-start = ((), (), s32[]{:S(2)}) async-start(), calls=%async_computation.10 | async-start | bytes 2621440 | tf_op jit(solution)/shard_map/reduce_scatter | solution.py:114
  148.7 52.8 %all-to-all-start.7 = ((bf16[128,2,4096]{2,1,0:T(2,128)(2,1)}), bf16[128,2,4096]{2,1,0:T(2,128)(2,1)S(1)}, u32[]{:S(2)}, u32[]{:S(2)}) async-start(bf16[128,2,4096]{2,1,0:T(2,128)(2,1)} %reshape.94), calls=%async_computation.8 | async-start | bytes 4194304 | tf_op jit(solution)/shard_map/all_to_all | solution.py:121
  201.5 7.5 %copy-start = (bf16[128,2,4096]{2,1,0:T(2,128)(2,1)}, bf16[128,2,4096]{2,1,0:T(2,128)(2,1)S(1)}, u32[]{:S(2)}) copy-start(bf16[128,2,4096]{2,1,0:T(2,128)(2,1)S(1)} %all-to-all-done.7) | copy-start | bytes 6291460
  201.5 19.1 %all-to-all-start.6 = ((bf16[32,2,4096]{2,1,0:T(2,128)(2,1)}), bf16[32,2,4096]{2,1,0:T(2,128)(2,1)S(1)}, u32[]{:S(2)}, u32[]{:S(2)}) async-start(bf16[32,2,4096]{2,1,0:T(2,128)(2,1)} %reshape.92), calls=%async_computation.7 | async-start | bytes 1048576 | tf_op jit(solution)/shard_map/all_to_all | solution.py:117
Sparse Core Ops, SparseCore 0:
  31.9 29.3 all-gather.1
  143.8 55.5 reduce-scatter.1
where the time goes:
time: 230 us; the launch traced here: 229 us
  waiting for transfers between devices  81.8 us (36%)
  starting transfers between devices  44.4 us (19%)
  blocking collectives  44.2 us (19%)
  local copies, waits for them, and re-layouts  31.6 us (14%)
  between operations  15 us (7%)
  matrix products  7.4 us (3%)
  other arithmetic  4.66 us (2%)
    reduce_scatter x1, waiting for transfers between devices, per_device(): lax.psum_scatter(query_part.astype(jnp.bfloat16), 'pa', scatter_dimension...  39.2 us
    all_to_all x1, blocking collectives, per_device(): lax.all_to_all(sent_q.reshape(n_rows, q_cap, emb_width), 'pb', split_axis...  20 us
    all_to_all x1, waiting for transfers between devices, per_device(): lax.all_to_all(sent_p.reshape(devices, p_cap, emb_width), ('pb', 'pa'), s...  14.3 us
    all_to_all x1, starting transfers between devices, per_device(): lax.all_to_all(passage_grad.reshape(devices, p_cap, emb_width), ('pb', 'p...  11.4 us
    unnamed x1, blocking collectives  10.7 us
    all_to_all x1, waiting for transfers between devices, per_device(): lax.all_to_all(sent_pcl.reshape(devices, p_cap), ('pb', 'pa'), split_axis...  7.85 us
    all_to_all x1, starting transfers between devices, per_device(): lax.all_to_all(query_sum.reshape(n_rows, q_cap, emb_width), 'pb', split_a...  7.47 us
    psum x1, blocking collectives, per_device(): row_total = lax.psum(jnp.sum(exp_terms, axis=1), 'pa')  6.89 us
  transfers between devices with their start and end apart: 9, of which 7 were waited for; matrix products, arithmetic and copies ran while one was open for 13% of the time, Pallas kernels for 0%

commit v1 on v0

v1 whole, which is shorter than its diff:
```python
import functools

import jax
import jax.numpy as jnp
from jax import lax
from jax.experimental import pallas as pl
from jax.experimental.pallas import tpu as pltpu
from jax.sharding import PartitionSpec as P

MESH = pl.DeviceIdType.MESH
F32, BF16, I32 = jnp.float32, jnp.bfloat16, jnp.int32
D = 4096
NB = 32
NZ = 4
QW = 512
PW = 2048
CT = 512
SCALE = 50.0
FILL = -1e30


def iota(shape, dim):
    return lax.broadcasted_iota(I32, shape, dim)


def shr(a, n):
    return lax.shift_right_logical(a, jnp.full(a.shape, n, I32))


def hot(cond):
    return jnp.where(cond, 1.0, 0.0).astype(BF16)


def nn(a, b):
    return lax.dot_general(a, b, (((1,), (0,)), ((), ())), preferred_element_type=F32)


def nt(a, b):
    return lax.dot_general(a, b, (((1,), (1,)), ((), ())), preferred_element_type=F32)


def tn(a, b):
    return lax.dot_general(a, b, (((0,), (0,)), ((), ())), preferred_element_type=F32)


def cols(j, width=CT):
    return pl.ds(pl.multiple_of(j * width, width), width)


def rows16(i):
    return pl.ds(pl.multiple_of(i * 16, 16), 16)


def kernel(
    q_ref, p_ref, ints_ref, allowed_ref, outq_ref, outp_ref,
    a_send, a_recv, b_send, b_recv, a_ret, a_back, b_ret, b_back,
    q_stack, p_stack, gq_stack, g_q, g_p, sel_q, allow_buf, q_meta, p_meta,
    q_all, p_all, score, part, part_in, gq_own, stat, stat_in,
    as_s, as_r, bs_s, bs_r, ar_s, ar_r, br_s, br_r, zq_s, zq_r, zs_s, zs_r, zg_s, zg_r,
):
    me = lax.axis_index("pb")
    z = lax.axis_index("pa")
    x, y, c = me // 8, (me // 2) % 4, me % 2

    def partner(i):
        dc, j = i // 16, i % 16
        g, dx = j // 4, j % 4
        dy = (dx + 4 - g) % 4
        return ((x + dx) % 4) * 8 + ((y + dy) % 4) * 2 + (c + dc) % 2

    barrier = pltpu.get_barrier_semaphore()

    def greet(i, carry):
        pl.semaphore_signal(barrier, inc=1, device_id=(partner(i), z), device_id_type=MESH)
        return carry

    lax.fori_loop(1, NB, greet, 0)
    for dz in range(1, NZ):
        pl.semaphore_signal(barrier, inc=1, device_id=(me, (z + dz) % NZ), device_id_type=MESH)

    ints = ints_ref[...]
    qc_row, pos_row, pc_row = ints[0:1, :], ints[1:2, :], ints[2:3, :]
    lane32, sub32 = iota((32, 256), 1), iota((32, 256), 0)
    qc_col = jnp.sum(jnp.where(lane32 == sub32, qc_row, 0), axis=1, keepdims=True)
    pos_col = jnp.sum(jnp.where(lane32 == sub32, pos_row, 0), axis=1, keepdims=True)
    qb_row, qb_col = shr(qc_row, 3), shr(qc_col, 3)
    q_before = jnp.where((qb_col == qb_row) & (sub32 < (lane32 & 31)), 1, 0)
    q_slot = qb_row * 2 + jnp.sum(q_before, axis=0, keepdims=True)
    lane128, sub128 = iota((128, 256), 1), iota((128, 256), 0)
    pc_col = jnp.sum(jnp.where(lane128 == sub128, pc_row, 0), axis=1, keepdims=True)
    pb_row, pb_col = shr(pc_row, 2), shr(pc_col, 2)
    p_before = jnp.where((pb_col == pb_row) & (sub128 < (lane128 & 127)), 1, 0)
    p_slot = pb_row * 2 + jnp.sum(p_before, axis=0, keepdims=True)

    big_r, big_c = iota((512, 256), 0), iota((512, 256), 1)
    g_q[...] = hot((q_slot == shr(big_r, 3)) & (shr(big_c, 5) == (big_r & 7)))
    g_p[...] = hot(
        (p_slot == shr(big_r, 4) * 8 + (big_r & 7)) & (shr(big_c, 7) == (shr(big_r, 3) & 1))
    )

    allow_buf[...] = jnp.zeros_like(allow_buf)
    allow_buf[:, 0:16] = allowed_ref[...].astype(F32).astype(BF16)
    reach = nn(hot(lane32 == qc_col), allow_buf[...])
    l32 = iota((32, 128), 1)
    q_num = jnp.where(l32 < 16, reach, 0.0)
    q_num = jnp.where(l32 == 16, (pos_col & 127).astype(F32) + 1.0, q_num)
    q_num = jnp.where(l32 == 17, shr(pos_col, 7).astype(F32), q_num).astype(BF16)
    l128, s128 = iota((128, 128), 1), iota((128, 128), 0)
    p_num = jnp.where((l128 < 16) & ((pc_col & 15) == l128), 1.0, 0.0)
    p_num = jnp.where(l128 == 16, s128.astype(F32) + 1.0, p_num).astype(BF16)
    mr_p, mr_q = iota((512, 128), 0), iota((512, 32), 0)
    gm_p = hot((p_slot[:, 0:128] == shr(mr_p, 4) * 8 + (mr_p & 15)) & ((mr_p & 15) < 8))
    gm_q = hot((q_slot[:, 0:32] == shr(mr_q, 4) * 2 + (mr_q & 15) - 8) & (shr(mr_q & 15, 1) == 4))
    a_send[:, QW:] = (nn(gm_p, p_num) + nn(gm_q, q_num)).astype(BF16)
    for e in range(8):
        q_stack[e * 32 : (e + 1) * 32, :] = q_ref[:, e * QW : (e + 1) * QW]
    a_send[:, 0:QW] = nn(g_q[...], q_stack[...]).astype(BF16)

    pl.semaphore_wait(barrier, NB - 1 + NZ - 1)

    def plane_copy(src, dst, send, recv, i, outgoing):
        d = partner(i)
        return pltpu.make_async_remote_copy(
            src_ref=src.at[rows16(d), :],
            dst_ref=dst.at[rows16(me if outgoing else d), :],
            send_sem=send.at[i],
            recv_sem=recv.at[me if outgoing else d],
            device_id=(d, z),
            device_id_type=MESH,
        )

    def start_all(src, dst, send, recv):
        def body(i, carry):
            plane_copy(src, dst, send, recv, i, True).start()
            return carry

        lax.fori_loop(1, NB, body, 0)

    def await_recv(src, dst, send, recv):
        def body(i, carry):
            plane_copy(src, dst, send, recv, i, False).wait_recv()
            return carry

        lax.fori_loop(1, NB, body, 0)

    def await_send(src, dst, send, recv):
        def body(i, carry):
            plane_copy(src, dst, send, recv, i, True).wait_send()
            return carry

        lax.fori_loop(1, NB, body, 0)

    def z_copy(src, dst, send, recv, dz):
        return pltpu.make_async_remote_copy(
            src_ref=src,
            dst_ref=dst,
            send_sem=send.at[dz - 1],
            recv_sem=recv.at[dz - 1],
            device_id=(me, (z + dz) % NZ),
            device_id_type=MESH,
        )

    mine = rows16(me)
    start_all(a_send, a_recv, as_s, as_r)
    a_recv[mine, :] = a_send[mine, :]

    p_stack[0:128, :] = p_ref[:, 0:PW]
    p_stack[128:256, :] = p_ref[:, PW:]

    def pack_p(j, carry):
        b_send[:, cols(j)] = nn(g_p[...], p_stack[:, cols(j)]).astype(BF16)
        return carry

    lax.fori_loop(0, PW // CT, pack_p, 0)
    start_all(b_send, b_recv, bs_s, bs_r)
    b_recv[mine, :] = b_send[mine, :]

    sr, sc = iota((512, 512), 0), iota((512, 512), 1)
    sel_q[...] = hot((shr(sr, 6) == (sc & 7)) & ((sr & 63) == shr(sc, 3)))
    hr, hc = iota((256, 512), 0), iota((256, 512), 1)
    half = (shr(hr, 3) == shr(hc, 4)) & ((hr & 7) == (hc & 7))
    sel_p0 = hot(half & ((hc & 8) == 0))
    sel_p1 = hot(half & ((hc & 8) == 8))
    nr, nc = iota((64, 512), 0), iota((64, 512), 1)
    sel_n = hot((shr(nr, 1) == shr(nc, 4)) & ((nc & 15) == 8 + (nr & 1)))

    await_recv(a_send, a_recv, as_s, as_r)
    zrows = pl.ds(pl.multiple_of(z * 64, 64), 64)
    whole = nn(sel_q[...], a_recv[:, 0:QW]).astype(BF16)
    for e in range(8):
        q_all[zrows, e * QW : (e + 1) * QW] = whole[e * 64 : (e + 1) * 64, :]
    q_all[zrows, D:] = nn(sel_n, a_recv[:, QW:]).astype(BF16)
    q_block = q_all.at[zrows, :]
    q_out = {dz: z_copy(q_block, q_block, zq_s, zq_r, dz) for dz in (1, 3, 2)}
    for dz in (1, 3, 2):
        q_out[dz].start()
    p_meta[...] = nn(sel_p0, a_recv[:, QW:]).astype(BF16)

    await_recv(b_send, b_recv, bs_s, bs_r)

    def unpack_p(j, carry):
        got = b_recv[:, cols(j)]
        p_all[:, cols(j)] = nn(sel_p0, got).astype(BF16)
        p_all[:, pl.ds(pl.multiple_of(PW + j * CT, CT), CT)] = nn(sel_p1, got).astype(BF16)
        return carry

    lax.fori_loop(0, PW // CT, unpack_p, 0)

    def z_from(dz):
        return (z + NZ - dz) % NZ

    for dz in (1, 3, 2):
        block = q_all.at[pl.ds(pl.multiple_of(z_from(dz) * 64, 64), 64), :]
        z_copy(block, block, zq_s, zq_r, dz).wait_recv()

    score[...] = jnp.zeros_like(score)

    def score_step(j, carry):
        score[...] += nt(p_all[:, cols(j)], q_all[:, cols(j)])
        return carry

    lax.fori_loop(0, D // CT, score_step, 0)
    qm, pm = q_all[:, D:], p_meta[...]
    l256 = iota((256, 128), 1)
    permitted = nt(jnp.where(l256 < 16, pm.astype(F32), 0.0).astype(BF16), qm) > 0.5
    er, el = iota((8, 128), 0), iota((8, 128), 1)
    q_dig = nt(hot((er < 2) & (el == 16 + er)), qm)
    q_lo, q_hi = q_dig[0:1, :], q_dig[1:2, :]
    q_code = jnp.where(q_lo > 0.5, q_hi * 256.0 + q_lo, -2.0)
    p_lo = pm[:, 16:17].astype(F32)
    p_dev = (shr(iota((256, 1), 0), 3) * NZ + z).astype(F32)
    p_code = jnp.where(p_lo > 0.5, p_dev * 256.0 + p_lo, -1.0)
    target = jnp.where(p_code == q_code, 1.0, 0.0)

    s = score[...] * SCALE
    top = jnp.max(jnp.where(permitted, s, FILL), axis=0, keepdims=True)
    total = jnp.sum(jnp.where(permitted, jnp.exp(s - top), 0.0), axis=0, keepdims=True)
    stat[0:1, :] = top
    stat[1:2, :] = total
    stat[2:8, :] = jnp.zeros((6, 256), F32)
    st_out = {dz: z_copy(stat, stat_in.at[dz - 1], zs_s, zs_r, dz) for dz in (1, 3, 2)}
    for dz in (1, 3, 2):
        st_out[dz].start()
    for dz in (1, 3, 2):
        st_out[dz].wait_recv()
    tops = [top] + [stat_in[i, 0:1, :] for i in range(3)]
    sums = [total] + [stat_in[i, 1:2, :] for i in range(3)]
    row_top = jnp.maximum(jnp.maximum(tops[0], tops[1]), jnp.maximum(tops[2], tops[3]))
    row_total = sum(l * jnp.exp(m - row_top) for m, l in zip(tops, sums))
    prob = jnp.where(permitted, jnp.exp(s - row_top), 0.0)
    prob = prob / jnp.where(row_total > 0.0, row_total, 1.0)
    gs = ((prob - target) * SCALE).astype(BF16)

    gs_t = jnp.transpose(gs.astype(F32)).astype(BF16)

    def part_step(j, carry):
        part[:, cols(j)] = nn(gs_t, p_all[:, cols(j)]).astype(BF16)
        return carry

    lax.fori_loop(0, D // CT, part_step, 0)
    pt_out = {}
    for dz in (1, 3, 2):
        rows = pl.ds(pl.multiple_of(((z + dz) % NZ) * 64, 64), 64)
        pt_out[dz] = z_copy(part.at[rows, :], part_in.at[dz - 1], zg_s, zg_r, dz)
        pt_out[dz].start()

    dr, dc_ = iota((512, 256), 0), iota((512, 256), 1)
    same = (shr(dr, 4) == shr(dc_, 3)) & ((dr & 7) == (dc_ & 7))
    gs0 = nn(hot(same & ((dr & 8) == 0)), gs).astype(BF16)
    gs1 = nn(hot(same & ((dr & 8) == 8)), gs).astype(BF16)

    def ret_step(j, carry):
        right = pl.ds(pl.multiple_of(PW + j * CT, CT), CT)
        b_ret[:, cols(j)] = (nn(gs0, q_all[:, cols(j)]) + nn(gs1, q_all[:, right])).astype(BF16)
        return carry

    lax.fori_loop(0, PW // CT, ret_step, 0)
    start_all(b_ret, b_back, br_s, br_r)
    b_back[mine, :] = b_ret[mine, :]

    for dz in (1, 3, 2):
        pt_out[dz].wait_recv()
    for e in range(8):
        ec = slice(e * QW, (e + 1) * QW)
        acc = part[zrows, ec].astype(F32)
        for i in range(3):
            acc = acc + part_in[i, :, ec].astype(F32)
        gq_stack[e * 64 : (e + 1) * 64, :] = acc.astype(BF16)
    a_ret[...] = tn(sel_q[...], gq_stack[...]).astype(BF16)
    start_all(a_ret, a_back, ar_s, ar_r)
    a_back[mine, :] = a_ret[mine, :]

    await_recv(b_ret, b_back, br_s, br_r)

    def out_p(j, carry):
        got = tn(g_p[...], b_back[:, cols(j)]).astype(BF16)
        outp_ref[:, cols(j)] = got[0:128, :]
        outp_ref[:, pl.ds(pl.multiple_of(PW + j * CT, CT), CT)] = got[128:256, :]
        return carry

    lax.fori_loop(0, PW // CT, out_p, 0)

    await_recv(a_ret, a_back, ar_s, ar_r)
    back = tn(g_q[...], a_back[...]).astype(BF16)
    for e in range(8):
        outq_ref[:, e * QW : (e + 1) * QW] = back[e * 32 : (e + 1) * 32, :]

    await_send(a_send, a_recv, as_s, as_r)
    await_send(b_send, b_recv, bs_s, bs_r)
    await_send(b_ret, b_back, br_s, br_r)
    await_send(a_ret, a_back, ar_s, ar_r)
    for dz in (1, 3, 2):
        q_out[dz].wait_send()
        st_out[dz].wait_send()
        pt_out[dz].wait_send()


def per_device(queries, passages, query_cluster, passage_cluster, allowed, positive):
    ints = jnp.concatenate(
        [
            jnp.tile(query_cluster, 8)[None],
            jnp.tile(positive, 8)[None],
            jnp.tile(passage_cluster, 2)[None],
            jnp.zeros((5, 256), I32),
        ],
        axis=0,
    )
    vm = pltpu.VMEM
    dma = pltpu.SemaphoreType.DMA
    return pl.pallas_call(
        kernel,
        out_shape=(
            jax.ShapeDtypeStruct(queries.shape, BF16),
            jax.ShapeDtypeStruct(passages.shape, BF16),
        ),
        in_specs=[pl.BlockSpec(memory_space=vm)] * 4,
        out_specs=(pl.BlockSpec(memory_space=vm),) * 2,
        scratch_shapes=[
            vm((512, QW + 128), BF16), vm((512, QW + 128), BF16),
            vm((512, PW), BF16), vm((512, PW), BF16),
            vm((512, QW), BF16), vm((512, QW), BF16),
            vm((512, PW), BF16), vm((512, PW), BF16),
            vm((256, QW), BF16), vm((256, PW), BF16), vm((512, QW), BF16),
            vm((512, 256), BF16), vm((512, 256), BF16), vm((512, 512), BF16),
            vm((256, 128), BF16), vm((64, 128), BF16), vm((256, 128), BF16),
            vm((256, D + 128), BF16), vm((256, D), BF16), vm((256, 256), F32),
            vm((256, D), BF16), vm((3, 64, D), BF16), vm((64, D), F32),
            vm((8, 256), F32), vm((3, 8, 256), F32),
        ]
        + [dma((NB,))] * 8
        + [dma((3,))] * 6,
        compiler_params=pltpu.CompilerParams(
            collective_id=0, has_side_effects=True, vmem_limit_bytes=56 * 1024 * 1024
        ),
        name="contrastive",
    )(queries, passages, ints, allowed)


def solution(mesh):
    rows = P(("pb", "pa"), None)
    flat = P(("pb", "pa"))
    return jax.shard_map(
        per_device,
        mesh=mesh,
        in_specs=(rows, rows, flat, flat, P(), flat),
        out_specs=(rows, rows),
        check_vma=False,
    )
```

time: 230 us -> 100 us (0.43)
  Pallas kernels: 0 us -> 92.6 us
  waiting for transfers between devices: 81.8 us -> 0 us
  starting transfers between devices: 44.4 us -> 0 us
  blocking collectives: 44.2 us -> 0 us
  local copies, waits for them, and re-layouts: 31.6 us -> 6.18 us
  between operations: 15 us -> 0.66 us
  matrix products: 7.4 us -> 0 us
  other arithmetic: 4.66 us -> 0.67 us
    pallas_call x0 -> x1, Pallas kernels: none -> 92.6 us  [per_device(): pl.pallas_call(kernel, out_shape=(jax.ShapeDtypeStruct(queries.shape, BF1...]
    all_to_all x7 -> x0, starting transfers between devices: 44.3 us -> none  [the longest x1 11.4 us: per_device(): lax.all_to_all(passage_grad.reshape(devices, p_cap, emb_width), ('pb', 'p...]
    all_to_all x7 -> x0, waiting for transfers between devices: 42.5 us -> none  [the longest x1 14.3 us: per_device(): lax.all_to_all(sent_p.reshape(devices, p_cap, emb_width), ('pb', 'pa'), s...]
    reduce_scatter x1 -> x0, waiting for transfers between devices: 39.2 us -> none  [per_device(): lax.psum_scatter(query_part.astype(jnp.bfloat16), 'pa', scatter_dimension...]
    all_to_all x1 -> x0, blocking collectives: 20 us -> none  [per_device(): lax.all_to_all(sent_q.reshape(n_rows, q_cap, emb_width), 'pb', split_axis...]
    reshape x11 -> x0, local copies, waits for them, and re-layouts: 14.9 us -> none  [the longest x1 2.75 us: per_device(): grad_passages = back_p.reshape(devices * p_cap, emb_width)[p_slot]]
    unnamed x1 -> x0, blocking collectives: 10.7 us -> none
    scatter x6 -> x0, local copies, waits for them, and re-layouts: 8.53 us -> none  [the longest x1 3.42 us: per_device(): jnp.zeros((devices * p_cap, emb_width), jnp.bfloat16).at[p_slot]]
  transfers between devices with their start and end apart: 9 -> 0, of which waited for: 7 -> 0; matrix products, arithmetic and copies ran while one was open for 13% -> 0% of each run, Pallas kernels for 0% -> 0%
where the time goes in v1:
time: 100 us
  Pallas kernels  92.6 us (93%)
  local copies, waits for them, and re-layouts  6.18 us (6%)
    pallas_call x1, Pallas kernels, per_device(): pl.pallas_call(kernel, out_shape=(jax.ShapeDtypeStruct(queries.shape, BF1...  92.6 us
    unnamed x11, local copies, waits for them, and re-layouts  5.94 us

profile of v1, /device:TPU:1, one launch (start us, length us, event | category | flops | bytes accessed | tf_op | source)
XLA Modules:
  0.0 100.2 jit_solution(16214851802569146292)
XLA Ops:
  0.6 0.0 copy-start.3
  0.7 0.1 pad.3.clone
  0.7 0.6 copy-done.3
  1.3 0.0 copy-start.1
  1.3 0.0 copy-start.2
  1.3 0.0 copy-start
  1.3 0.6 copy-done.1
  2.0 0.1 broadcast_in_dim_tile.9
  2.0 0.0 copy-done.2
  2.0 0.1 broadcast_in_dim_tile.10
  2.1 0.7 add_add_fusion.ints_ref
  2.8 0.0 copy-done
  2.8 0.8 copy.8.allowed_ref
  3.5 92.6 %contrastive.1 = (bf16[32,4096]{1,0:T(8,128)(2,1)}, bf16[128,4096]{1,0:T(8,128)(2,1)}) custom-call(bf16[32,4096]{1,0:T(8,128)(2,1)} %q_ref.1, bf16[128,4096]{1,0:T(8,128)(2,1)} %p_ref.1, s32[8,256]{1,0:T(8,128)} %add_add_fusion.ints_ref, s32[256,16]{1,0:T(8,128)} %copy.8.allowed_ref), custom_call_target="tpu_custom_call" | custom-call | tf_op jit(solution)/shard_map/contrastive/pallas_call | solution.py:330
  96.2 1.7 %copy.11 = bf16[32,4096]{1,0:T(8,128)(2,1)} copy(bf16[32,4096]{1,0:T(8,128)(2,1)} %get-tuple-element.4) | data formatting | bytes 524288
  97.9 2.3 %copy.12 = bf16[128,4096]{1,0:T(8,128)(2,1)} copy(bf16[128,4096]{1,0:T(8,128)(2,1)} %get-tuple-element.5) | data formatting | bytes 2097152
  (4 shorter events, 0.0 us)
Async XLA Ops:
  0.6 0.7 copy-start.3
  1.3 0.7 copy-start.1
  1.3 0.7 copy-start.2
  1.3 1.5 %copy-start = (s32[256,16]{0,1:T(8,128)S(1)}, s32[256,16]{0,1:T(8,128)}, u32[]{:S(2)}) copy-start(s32[256,16]{0,1:T(8,128)} %param.10) | copy-start | bytes 49156

commit v2 on v1

--- a/solution.py
+++ b/solution.py
@@ -52,11 +52,12 @@
 
 
 def kernel(
-    q_ref, p_ref, ints_ref, allowed_ref, outq_ref, outp_ref,
-    a_send, a_recv, b_send, b_recv, a_ret, a_back, b_ret, b_back,
-    q_stack, p_stack, gq_stack, g_q, g_p, sel_q, allow_buf, q_meta, p_meta,
-    q_all, p_all, score, part, part_in, gq_own, stat, stat_in,
-    as_s, as_r, bs_s, bs_r, ar_s, ar_r, br_s, br_r, zq_s, zq_r, zs_s, zs_r, zg_s, zg_r,
+    q_hbm, p_hbm, qc_hbm, pos_hbm, pc_hbm, allowed_hbm,
+    a_back, b_back, g_q, g_p,
+    a_send, a_recv, b_send, b_recv, a_ret, b_ret,
+    q_stack, p_stack, gq_stack, sel_q, allow_int, allow_buf, qc_buf, pos_buf, pc_buf, p_meta,
+    q_all, p_all, score, part, relay_in, part_in, stat, stat_in,
+    as_s, as_r, bs_s, bs_r, ar_s, ar_r, br_s, br_r, zq_s, zq_r, zs_s, zs_r, zg_s, zg_r, in_sem,
 ):
     me = lax.axis_index("pb")
     z = lax.axis_index("pa")
@@ -68,6 +69,31 @@
         dy = (dx + 4 - g) % 4
         return ((x + dx) % 4) * 8 + ((y + dy) % 4) * 2 + (c + dc) % 2
 
+    loads = [
+        pltpu.make_async_copy(qc_hbm, qc_buf, in_sem.at[0]),
+        pltpu.make_async_copy(pos_hbm, pos_buf, in_sem.at[1]),
+        pltpu.make_async_copy(pc_hbm, pc_buf, in_sem.at[2]),
+        pltpu.make_async_copy(allowed_hbm, allow_int, in_sem.at[3]),
+    ]
+    for e in range(8):
+        loads.append(
+            pltpu.make_async_copy(
+                q_hbm.at[:, e * QW : (e + 1) * QW],
+                q_stack.at[e * 32 : (e + 1) * 32, :],
+                in_sem.at[4 + e],
+            )
+        )
+    for h in range(2):
+        loads.append(
+            pltpu.make_async_copy(
+                p_hbm.at[:, h * PW : (h + 1) * PW],
+                p_stack.at[h * 128 : (h + 1) * 128, :],
+                in_sem.at[12 + h],
+            )
+        )
+    for load in loads:
+        load.start()
+
     barrier = pltpu.get_barrier_semaphore()
 
     def greet(i, carry):
@@ -78,42 +104,48 @@
     for dz in range(1, NZ):
         pl.semaphore_signal(barrier, inc=1, device_id=(me, (z + dz) % NZ), device_id_type=MESH)
 
-    ints = ints_ref[...]
-    qc_row, pos_row, pc_row = ints[0:1, :], ints[1:2, :], ints[2:3, :]
-    lane32, sub32 = iota((32, 256), 1), iota((32, 256), 0)
+    for load in loads[:4]:
+        load.wait()
+    qc_row, pos_row, pc_row = qc_buf[...], pos_buf[...], pc_buf[...]
+    lane32, sub32 = iota((32, 32), 1), iota((32, 32), 0)
     qc_col = jnp.sum(jnp.where(lane32 == sub32, qc_row, 0), axis=1, keepdims=True)
     pos_col = jnp.sum(jnp.where(lane32 == sub32, pos_row, 0), axis=1, keepdims=True)
     qb_row, qb_col = shr(qc_row, 3), shr(qc_col, 3)
-    q_before = jnp.where((qb_col == qb_row) & (sub32 < (lane32 & 31)), 1, 0)
+    q_before = jnp.where((qb_col == qb_row) & (sub32 < lane32), 1, 0)
     q_slot = qb_row * 2 + jnp.sum(q_before, axis=0, keepdims=True)
-    lane128, sub128 = iota((128, 256), 1), iota((128, 256), 0)
+    lane128, sub128 = iota((128, 128), 1), iota((128, 128), 0)
     pc_col = jnp.sum(jnp.where(lane128 == sub128, pc_row, 0), axis=1, keepdims=True)
     pb_row, pb_col = shr(pc_row, 2), shr(pc_col, 2)
-    p_before = jnp.where((pb_col == pb_row) & (sub128 < (lane128 & 127)), 1, 0)
+    p_before = jnp.where((pb_col == pb_row) & (sub128 < lane128), 1, 0)
     p_slot = pb_row * 2 + jnp.sum(p_before, axis=0, keepdims=True)
 
+    spread = hot(iota((32, 256), 0) == (iota((32, 256), 1) & 31))
+    q_slot8 = nn(jnp.broadcast_to(q_slot, (8, 32)).astype(F32).astype(BF16), spread)[0:1, :]
     big_r, big_c = iota((512, 256), 0), iota((512, 256), 1)
-    g_q[...] = hot((q_slot == shr(big_r, 3)) & (shr(big_c, 5) == (big_r & 7)))
-    g_p[...] = hot(
-        (p_slot == shr(big_r, 4) * 8 + (big_r & 7)) & (shr(big_c, 7) == (shr(big_r, 3) & 1))
+    g_q[...] = hot(
+        (q_slot8 == shr(big_r, 3).astype(F32)) & (shr(big_c, 5) == (big_r & 7))
     )
+    half_r = iota((512, 128), 0)
+    here = p_slot == shr(half_r, 4) * 8 + (half_r & 7)
+    g_p[:, 0:128] = hot(here & ((half_r & 8) == 0))
+    g_p[:, 128:256] = hot(here & ((half_r & 8) == 8))
 
     allow_buf[...] = jnp.zeros_like(allow_buf)
-    allow_buf[:, 0:16] = allowed_ref[...].astype(F32).astype(BF16)
-    reach = nn(hot(lane32 == qc_col), allow_buf[...])
+    allow_buf[0:16, :] = allow_int[...].astype(F32).astype(BF16)
+    l256c = iota((32, 256), 1)
+    reach = nt(hot(l256c == qc_col), allow_buf[...])
     l32 = iota((32, 128), 1)
     q_num = jnp.where(l32 < 16, reach, 0.0)
     q_num = jnp.where(l32 == 16, (pos_col & 127).astype(F32) + 1.0, q_num)
     q_num = jnp.where(l32 == 17, shr(pos_col, 7).astype(F32), q_num).astype(BF16)
-    l128, s128 = iota((128, 128), 1), iota((128, 128), 0)
-    p_num = jnp.where((l128 < 16) & ((pc_col & 15) == l128), 1.0, 0.0)
-    p_num = jnp.where(l128 == 16, s128.astype(F32) + 1.0, p_num).astype(BF16)
+    p_num = jnp.where((lane128 < 16) & ((pc_col & 15) == lane128), 1.0, 0.0)
+    p_num = jnp.where(lane128 == 16, sub128.astype(F32) + 1.0, p_num).astype(BF16)
     mr_p, mr_q = iota((512, 128), 0), iota((512, 32), 0)
-    gm_p = hot((p_slot[:, 0:128] == shr(mr_p, 4) * 8 + (mr_p & 15)) & ((mr_p & 15) < 8))
-    gm_q = hot((q_slot[:, 0:32] == shr(mr_q, 4) * 2 + (mr_q & 15) - 8) & (shr(mr_q & 15, 1) == 4))
+    gm_p = hot((p_slot == shr(mr_p, 4) * 8 + (mr_p & 15)) & ((mr_p & 15) < 8))
+    gm_q = hot((q_slot == shr(mr_q, 4) * 2 + (mr_q & 15) - 8) & (shr(mr_q & 15, 1) == 4))
     a_send[:, QW:] = (nn(gm_p, p_num) + nn(gm_q, q_num)).astype(BF16)
-    for e in range(8):
-        q_stack[e * 32 : (e + 1) * 32, :] = q_ref[:, e * QW : (e + 1) * QW]
+    for load in loads[4:12]:
+        load.wait()
     a_send[:, 0:QW] = nn(g_q[...], q_stack[...]).astype(BF16)
 
     pl.semaphore_wait(barrier, NB - 1 + NZ - 1)
@@ -150,22 +182,26 @@
 
         lax.fori_loop(1, NB, body, 0)
 
-    def z_copy(src, dst, send, recv, dz):
+    def z_copy(src, dst, send, recv, dz, k=None):
+        k = dz - 1 if k is None else k
         return pltpu.make_async_remote_copy(
             src_ref=src,
             dst_ref=dst,
-            send_sem=send.at[dz - 1],
-            recv_sem=recv.at[dz - 1],
+            send_sem=send.at[k],
+            recv_sem=recv.at[k],
             device_id=(me, (z + dz) % NZ),
             device_id_type=MESH,
         )
 
+    def block_rows(dz):
+        return pl.ds(pl.multiple_of(((z + dz) % NZ) * 64, 64), 64)
+
     mine = rows16(me)
     start_all(a_send, a_recv, as_s, as_r)
     a_recv[mine, :] = a_send[mine, :]
 
-    p_stack[0:128, :] = p_ref[:, 0:PW]
-    p_stack[128:256, :] = p_ref[:, PW:]
+    for load in loads[12:]:
+        load.wait()
 
     def pack_p(j, carry):
         b_send[:, cols(j)] = nn(g_p[...], p_stack[:, cols(j)]).astype(BF16)
@@ -190,11 +226,23 @@
     for e in range(8):
         q_all[zrows, e * QW : (e + 1) * QW] = whole[e * 64 : (e + 1) * 64, :]
     q_all[zrows, D:] = nn(sel_n, a_recv[:, QW:]).astype(BF16)
-    q_block = q_all.at[zrows, :]
-    q_out = {dz: z_copy(q_block, q_block, zq_s, zq_r, dz) for dz in (1, 3, 2)}
-    for dz in (1, 3, 2):
-        q_out[dz].start()
+    left, right = slice(0, PW), slice(PW, D + 128)
+
+    def q_hop(dz_block, columns, dz, k):
+        piece = q_all.at[block_rows(dz_block), columns]
+        return z_copy(piece, piece, zq_s, zq_r, dz, k)
+
+    q_out = [
+        q_hop(0, left, 1, 0), q_hop(0, right, 3, 3), q_hop(0, right, 1, 1), q_hop(0, left, 3, 4),
+        q_hop(3, left, 1, 2), q_hop(1, right, 3, 5),
+    ]
+    for copy in q_out[:4]:
+        copy.start()
     p_meta[...] = nn(sel_p0, a_recv[:, QW:]).astype(BF16)
+    q_hop(3, left, 1, 0).wait_recv()
+    q_out[4].start()
+    q_hop(1, right, 3, 3).wait_recv()
+    q_out[5].start()
 
     await_recv(b_send, b_recv, bs_s, bs_r)
 
@@ -206,12 +254,10 @@
 
     lax.fori_loop(0, PW // CT, unpack_p, 0)
 
-    def z_from(dz):
-        return (z + NZ - dz) % NZ
-
-    for dz in (1, 3, 2):
-        block = q_all.at[pl.ds(pl.multiple_of(z_from(dz) * 64, 64), 64), :]
-        z_copy(block, block, zq_s, zq_r, dz).wait_recv()
+    q_hop(3, right, 1, 1).wait_recv()
+    q_hop(1, left, 3, 4).wait_recv()
+    q_hop(2, left, 1, 2).wait_recv()
+    q_hop(2, right, 3, 5).wait_recv()
 
     score[...] = jnp.zeros_like(score)
 
@@ -251,19 +297,6 @@
     prob = prob / jnp.where(row_total > 0.0, row_total, 1.0)
     gs = ((prob - target) * SCALE).astype(BF16)
 
-    gs_t = jnp.transpose(gs.astype(F32)).astype(BF16)
-
-    def part_step(j, carry):
-        part[:, cols(j)] = nn(gs_t, p_all[:, cols(j)]).astype(BF16)
-        return carry
-
-    lax.fori_loop(0, D // CT, part_step, 0)
-    pt_out = {}
-    for dz in (1, 3, 2):
-        rows = pl.ds(pl.multiple_of(((z + dz) % NZ) * 64, 64), 64)
-        pt_out[dz] = z_copy(part.at[rows, :], part_in.at[dz - 1], zg_s, zg_r, dz)
-        pt_out[dz].start()
-
     dr, dc_ = iota((512, 256), 0), iota((512, 256), 1)
     same = (shr(dr, 4) == shr(dc_, 3)) & ((dr & 7) == (dc_ & 7))
     gs0 = nn(hot(same & ((dr & 8) == 0)), gs).astype(BF16)
@@ -278,12 +311,42 @@
     start_all(b_ret, b_back, br_s, br_r)
     b_back[mine, :] = b_ret[mine, :]
 
-    for dz in (1, 3, 2):
-        pt_out[dz].wait_recv()
+    gs_t = jnp.transpose(gs.astype(F32)).astype(BF16)
+
+    def part_step(j, carry):
+        part[:, cols(j)] = nn(gs_t, p_all[:, cols(j)]).astype(BF16)
+        return carry
+
+    lax.fori_loop(0, D // CT, part_step, 0)
+    low, high = slice(0, PW), slice(PW, D)
+
+    def part_hop(dz_block, columns, dst, dz, k):
+        return z_copy(part.at[block_rows(dz_block), columns], dst, zg_s, zg_r, dz, k)
+
+    pt_out = [
+        part_hop(2, low, relay_in.at[0], 1, 0),
+        part_hop(2, high, relay_in.at[1], 3, 1),
+        part_hop(1, high, part_in.at[0, :, high], 1, 2),
+        part_hop(3, low, part_in.at[1, :, low], 3, 3),
+        part_hop(1, low, part_in.at[0, :, low], 1, 4),
+        part_hop(3, high, part_in.at[1, :, high], 3, 5),
+    ]
+    for copy in pt_out[:4]:
+        copy.start()
+    pt_out[0].wait_recv()
+    up = part[block_rows(1), low].astype(F32) + relay_in[0].astype(F32)
+    part[block_rows(1), low] = up.astype(BF16)
+    pt_out[4].start()
+    pt_out[1].wait_recv()
+    down = part[block_rows(3), high].astype(F32) + relay_in[1].astype(F32)
+    part[block_rows(3), high] = down.astype(BF16)
+    pt_out[5].start()
+    for copy in pt_out[2:]:
+        copy.wait_recv()
     for e in range(8):
         ec = slice(e * QW, (e + 1) * QW)
         acc = part[zrows, ec].astype(F32)
-        for i in range(3):
+        for i in range(2):
             acc = acc + part_in[i, :, ec].astype(F32)
         gq_stack[e * 64 : (e + 1) * 64, :] = acc.astype(BF16)
     a_ret[...] = tn(sel_q[...], gq_stack[...]).astype(BF16)
@@ -291,69 +354,96 @@
     a_back[mine, :] = a_ret[mine, :]
 
     await_recv(b_ret, b_back, br_s, br_r)
-
-    def out_p(j, carry):
-        got = tn(g_p[...], b_back[:, cols(j)]).astype(BF16)
-        outp_ref[:, cols(j)] = got[0:128, :]
-        outp_ref[:, pl.ds(pl.multiple_of(PW + j * CT, CT), CT)] = got[128:256, :]
-        return carry
-
-    lax.fori_loop(0, PW // CT, out_p, 0)
-
     await_recv(a_ret, a_back, ar_s, ar_r)
-    back = tn(g_q[...], a_back[...]).astype(BF16)
-    for e in range(8):
-        outq_ref[:, e * QW : (e + 1) * QW] = back[e * 32 : (e + 1) * 32, :]
 
     await_send(a_send, a_recv, as_s, as_r)
     await_send(b_send, b_recv, bs_s, bs_r)
     await_send(b_ret, b_back, br_s, br_r)
     await_send(a_ret, a_back, ar_s, ar_r)
+    for copy in q_out + pt_out:
+        copy.wait_send()
     for dz in (1, 3, 2):
-        q_out[dz].wait_send()
         st_out[dz].wait_send()
-        pt_out[dz].wait_send()
+
+
+def unpack(a_back, b_back, g_q, g_p, outq_hbm, outp_hbm, q_buf, p_buf, sem):
+    copies = []
+    for j in range(PW // CT):
+        got = tn(g_p[...], b_back[:, j * CT : (j + 1) * CT]).astype(BF16)
+        for h in range(2):
+            columns = slice(h * PW + j * CT, h * PW + (j + 1) * CT)
+            p_buf[:, columns] = got[h * 128 : (h + 1) * 128, :]
+            copy = pltpu.make_async_copy(
+                p_buf.at[:, columns], outp_hbm.at[:, columns], sem.at[2 * j + h]
+            )
+            copy.start()
+            copies.append(copy)
+    back = tn(g_q[...], a_back[...]).astype(BF16)
+    for e in range(8):
+        q_buf[:, e * QW : (e + 1) * QW] = back[e * 32 : (e + 1) * 32, :]
+    copy = pltpu.make_async_copy(q_buf, outq_hbm, sem.at[8])
+    copy.start()
+    for c in copies + [copy]:
+        c.wait()
 
 
 def per_device(queries, passages, query_cluster, passage_cluster, allowed, positive):
-    ints = jnp.concatenate(
-        [
-            jnp.tile(query_cluster, 8)[None],
-            jnp.tile(positive, 8)[None],
-            jnp.tile(passage_cluster, 2)[None],
-            jnp.zeros((5, 256), I32),
-        ],
-        axis=0,
-    )
     vm = pltpu.VMEM
     dma = pltpu.SemaphoreType.DMA
+    hbm = pl.BlockSpec(memory_space=pl.ANY)
+    res = pl.BlockSpec(memory_space=vm)
+    landed = pl.pallas_call(
+        kernel,
+        out_shape=(
+            pltpu.VMEM((512, QW), BF16),
+            pltpu.VMEM((512, PW), BF16),
+            pltpu.VMEM((512, 256), BF16),
+            pltpu.VMEM((512, 256), BF16),
+        ),
+        in_specs=[pl.BlockSpec(memory_space=pltpu.HBM)] * 6,
+        out_specs=(res,) * 4,
+        scratch_shapes=[
+            vm((512, QW + 128), BF16), vm((512, QW + 128), BF16),
+            vm((512, PW), BF16), vm((512, PW), BF16),
+            vm((512, QW), BF16), vm((512, PW), BF16),
+            vm((256, QW), BF16), vm((256, PW), BF16), vm((512, QW), BF16),
+            vm((512, 512), BF16),
+            vm((16, 256), I32), vm((128, 256), BF16),
+            vm((1, 32), I32), vm((1, 32), I32), vm((1, 128), I32),
+            vm((256, 128), BF16),
+            vm((256, D + 128), BF16), vm((256, D), BF16), vm((256, 256), F32),
+            vm((256, D), BF16), vm((2, 64, PW), BF16), vm((2, 64, D), BF16),
+            vm((8, 256), F32), vm((3, 8, 256), F32),
+        ]
+        + [dma((NB,))] * 8
+        + [dma((6,))] * 2
+        + [dma((3,))] * 2
+        + [dma((6,))] * 2
+        + [dma((14,))],
+        compiler_params=pltpu.CompilerParams(
+            collective_id=0, has_side_effects=True, vmem_limit_bytes=54 * 1024 * 1024
+        ),
+        name="contrastive",
+    )(
+        queries,
+        passages,
+        query_cluster.reshape(1, -1),
+        positive.reshape(1, -1),
+        passage_cluster.reshape(1, -1),
+        allowed.T,
+    )
     return pl.pallas_call(
-        kernel,
+        unpack,
         out_shape=(
             jax.ShapeDtypeStruct(queries.shape, BF16),
             jax.ShapeDtypeStruct(passages.shape, BF16),
         ),
-        in_specs=[pl.BlockSpec(memory_space=vm)] * 4,
-        out_specs=(pl.BlockSpec(memory_space=vm),) * 2,
-        scratch_shapes=[
-            vm((512, QW + 128), BF16), vm((512, QW + 128), BF16),
-            vm((512, PW), BF16), vm((512, PW), BF16),
-            vm((512, QW), BF16), vm((512, QW), BF16),
-            vm((512, PW), BF16), vm((512, PW), BF16),
-            vm((256, QW), BF16), vm((256, PW), BF16), vm((512, QW), BF16),
-            vm((512, 256), BF16), vm((512, 256), BF16), vm((512, 512), BF16),
-            vm((256, 128), BF16), vm((64, 128), BF16), vm((256, 128), BF16),
-            vm((256, D + 128), BF16), vm((256, D), BF16), vm((256, 256), F32),
-            vm((256, D), BF16), vm((3, 64, D), BF16), vm((64, D), F32),
-            vm((8, 256), F32), vm((3, 8, 256), F32),
-        ]
-        + [dma((NB,))] * 8
-        + [dma((3,))] * 6,
-        compiler_params=pltpu.CompilerParams(
-            collective_id=0, has_side_effects=True, vmem_limit_bytes=56 * 1024 * 1024
-        ),
-        name="contrastive",
-    )(queries, passages, ints, allowed)
+        in_specs=[res] * 4,
+        out_specs=(hbm, hbm),
+        scratch_shapes=[vm((32, D), BF16), vm((128, D), BF16), dma((9,))],
+        compiler_params=pltpu.CompilerParams(vmem_limit_bytes=16 * 1024 * 1024),
+        name="unpack",
+    )(*landed)
 
 
 def solution(mesh):

time: 100 us -> 90.6 us (0.906)
  local copies, waits for them, and re-layouts: 6.18 us -> 0 us
  Pallas kernels: 92.6 us -> 89.8 us
    unnamed x11 -> x0, local copies, waits for them, and re-layouts: 5.94 us -> none
    pallas_call x1 -> x2, Pallas kernels: 92.6 us -> 89.8 us  [the longest x1 88.2 us: per_device(): pl.pallas_call(kernel, out_shape=(pltpu.VMEM((512, QW), BF16), pltpu.VMEM...]
where the time goes in v2:
time: 90.6 us; the launch traced here: 90.5 us
  Pallas kernels  89.8 us (99%)
    pallas_call x1, Pallas kernels, per_device(): pl.pallas_call(kernel, out_shape=(pltpu.VMEM((512, QW), BF16), pltpu.VMEM...  88.2 us

profile of v2, /device:TPU:1, one launch (start us, length us, event | category | flops | bytes accessed | tf_op | source)
XLA Modules:
  0.0 90.5 jit_solution(11721588602929985936)
XLA Ops:
  0.6 88.2 %contrastive.1 = (bf16[512,512]{1,0:T(8,128)(2,1)S(1)}, bf16[512,2048]{1,0:T(8,128)(2,1)S(1)}, bf16[512,256]{1,0:T(8,128)(2,1)S(1)}, bf16[512,256]{1,0:T(8,128)(2,1)S(1)}) custom-call(bf16[32,4096]{1,0:T(8,128)(2,1)} %q_hbm.1, bf16[128,4096]{1,0:T(8,128)(2,1)} %p_hbm.1, s32[1,32]{1,0:T(1,128)} %bitcast.5, s32[1,32]{1,0:T(1,128)} %bitcast.6, ...), custom_call_target="tpu_custom_call" | custom-call | tf_op jit(solution)/shard_map/contrastive/pallas_call | solution.py:395
  88.8 1.7 %unpack.1 = (bf16[32,4096]{1,0:T(8,128)(2,1)}, bf16[128,4096]{1,0:T(8,128)(2,1)}) custom-call(bf16[512,512]{1,0:T(8,128)(2,1)S(1)} %get-tuple-element.6.a_back, bf16[512,2048]{1,0:T(8,128)(2,1)S(1)} %get-tuple-element.7.b_back, bf16[512,256]{1,0:T(8,128)(2,1)S(1)} %get-tuple-element.8.g_q, bf16[512,256]{1,0:T(8,128)(2,1)S(1)} %get-tuple-element.9.g_p), custom_call_target="tpu_custom_call" | custom-call | tf_op jit(solution)/shard_map/unpack/pallas_call | solution.py:435

commit v3 on v2

--- a/solution.py
+++ b/solution.py
@@ -56,18 +56,25 @@
     a_back, b_back, g_q, g_p,
     a_send, a_recv, b_send, b_recv, a_ret, b_ret,
     q_stack, p_stack, gq_stack, sel_q, allow_int, allow_buf, qc_buf, pos_buf, pc_buf, p_meta,
-    q_all, p_all, score, part, relay_in, part_in, stat, stat_in,
+    q_all, p_all, score, live, target, gs, part, relay_in, part_in, stat, stat_in,
     as_s, as_r, bs_s, bs_r, ar_s, ar_r, br_s, br_r, zq_s, zq_r, zs_s, zs_r, zg_s, zg_r, in_sem,
 ):
     me = lax.axis_index("pb")
     z = lax.axis_index("pa")
     x, y, c = me // 8, (me // 2) % 4, me % 2
 
+    def offset(i):
+        j = i % 16
+        dx = j % 4
+        return dx, (dx + 4 - j // 4) % 4, i // 16
+
     def partner(i):
-        dc, j = i // 16, i % 16
-        g, dx = j // 4, j % 4
-        dy = (dx + 4 - g) % 4
+        dx, dy, dc = offset(i)
         return ((x + dx) % 4) * 8 + ((y + dy) % 4) * 2 + (c + dc) % 2
+
+    def origin(i):
+        dx, dy, dc = offset(i)
+        return ((x + 4 - dx) % 4) * 8 + ((y + 4 - dy) % 4) * 2 + (c + dc) % 2
 
     loads = [
         pltpu.make_async_copy(qc_hbm, qc_buf, in_sem.at[0]),
@@ -150,37 +157,38 @@
 
     pl.semaphore_wait(barrier, NB - 1 + NZ - 1)
 
-    def plane_copy(src, dst, send, recv, i, outgoing):
+    def out_copy(src, dst, send, recv, i):
         d = partner(i)
         return pltpu.make_async_remote_copy(
             src_ref=src.at[rows16(d), :],
-            dst_ref=dst.at[rows16(me if outgoing else d), :],
+            dst_ref=dst.at[rows16(i), :],
             send_sem=send.at[i],
-            recv_sem=recv.at[me if outgoing else d],
+            recv_sem=recv.at[i],
             device_id=(d, z),
             device_id_type=MESH,
         )
 
-    def start_all(src, dst, send, recv):
+    def back_copy(src, dst, send, recv, i, place):
+        return pltpu.make_async_remote_copy(
+            src_ref=src.at[rows16(i), :],
+            dst_ref=dst.at[rows16(place), :],
+            send_sem=send.at[i],
+            recv_sem=recv.at[i],
+            device_id=(origin(i), z),
+            device_id_type=MESH,
+        )
+
+    def steps(lo, hi, act):
         def body(i, carry):
-            plane_copy(src, dst, send, recv, i, True).start()
+            act(i)
             return carry
 
-        lax.fori_loop(1, NB, body, 0)
-
-    def await_recv(src, dst, send, recv):
-        def body(i, carry):
-            plane_copy(src, dst, send, recv, i, False).wait_recv()
-            return carry
-
-        lax.fori_loop(1, NB, body, 0)
-
-    def await_send(src, dst, send, recv):
-        def body(i, carry):
-            plane_copy(src, dst, send, recv, i, True).wait_send()
-            return carry
-
-        lax.fori_loop(1, NB, body, 0)
+        lax.fori_loop(lo, hi, body, 0)
+
+    a_out = functools.partial(out_copy, a_send, a_recv, as_s, as_r)
+    b_out = functools.partial(out_copy, b_send, b_recv, bs_s, bs_r)
+    a_home = functools.partial(back_copy, a_ret, a_back, ar_s, ar_r)
+    b_home = functools.partial(back_copy, b_ret, b_back, br_s, br_r)
 
     def z_copy(src, dst, send, recv, dz, k=None):
         k = dz - 1 if k is None else k
@@ -197,8 +205,8 @@
         return pl.ds(pl.multiple_of(((z + dz) % NZ) * 64, 64), 64)
 
     mine = rows16(me)
-    start_all(a_send, a_recv, as_s, as_r)
-    a_recv[mine, :] = a_send[mine, :]
+    steps(1, NB, lambda i: a_out(i).start())
+    a_recv[0:16, :] = a_send[mine, :]
 
     for load in loads[12:]:
         load.wait()
@@ -208,19 +216,18 @@
         return carry
 
     lax.fori_loop(0, PW // CT, pack_p, 0)
-    start_all(b_send, b_recv, bs_s, bs_r)
-    b_recv[mine, :] = b_send[mine, :]
+    steps(1, NB, lambda i: b_out(i).start())
+    b_recv[0:16, :] = b_send[mine, :]
 
     sr, sc = iota((512, 512), 0), iota((512, 512), 1)
     sel_q[...] = hot((shr(sr, 6) == (sc & 7)) & ((sr & 63) == shr(sc, 3)))
     hr, hc = iota((256, 512), 0), iota((256, 512), 1)
     half = (shr(hr, 3) == shr(hc, 4)) & ((hr & 7) == (hc & 7))
-    sel_p0 = hot(half & ((hc & 8) == 0))
-    sel_p1 = hot(half & ((hc & 8) == 8))
+    sel_m = hot(half & ((hc & 8) == 0))
     nr, nc = iota((64, 512), 0), iota((64, 512), 1)
     sel_n = hot((shr(nr, 1) == shr(nc, 4)) & ((nc & 15) == 8 + (nr & 1)))
 
-    await_recv(a_send, a_recv, as_s, as_r)
+    steps(1, NB, lambda i: a_out(i).wait_recv())
     zrows = pl.ds(pl.multiple_of(z * 64, 64), 64)
     whole = nn(sel_q[...], a_recv[:, 0:QW]).astype(BF16)
     for e in range(8):
@@ -238,54 +245,67 @@
     ]
     for copy in q_out[:4]:
         copy.start()
-    p_meta[...] = nn(sel_p0, a_recv[:, QW:]).astype(BF16)
+    p_meta[...] = nn(sel_m, a_recv[:, QW:]).astype(BF16)
     q_hop(3, left, 1, 0).wait_recv()
     q_out[4].start()
     q_hop(1, right, 3, 3).wait_recv()
     q_out[5].start()
 
-    await_recv(b_send, b_recv, bs_s, bs_r)
-
-    def unpack_p(j, carry):
-        got = b_recv[:, cols(j)]
-        p_all[:, cols(j)] = nn(sel_p0, got).astype(BF16)
-        p_all[:, pl.ds(pl.multiple_of(PW + j * CT, CT), CT)] = nn(sel_p1, got).astype(BF16)
-        return carry
-
-    lax.fori_loop(0, PW // CT, unpack_p, 0)
+    ur, uc = iota((64, 128), 0), iota((64, 128), 1)
+    pair = (shr(ur, 3) == shr(uc, 4)) & ((ur & 7) == (uc & 7))
+    sel_u = [hot(pair & ((uc & 8) == 8 * h)) for h in range(2)]
+
+    def arrive(g, lo):
+        steps(lo, 8 * (g + 1), lambda i: b_out(i).wait_recv())
+        for j in range(PW // CT):
+            got = b_recv[g * 128 : (g + 1) * 128, j * CT : (j + 1) * CT]
+            for h in range(2):
+                columns = slice(h * PW + j * CT, h * PW + (j + 1) * CT)
+                p_all[g * 64 : (g + 1) * 64, columns] = nn(sel_u[h], got).astype(BF16)
+
+    def score_rows(lo, hi):
+        acc = nt(p_all[lo:hi, 0:CT], q_all[:, 0:CT])
+        for j in range(1, D // CT):
+            acc = acc + nt(p_all[lo:hi, j * CT : (j + 1) * CT], q_all[:, j * CT : (j + 1) * CT])
+        score[lo:hi, :] = acc * SCALE
+
+    for g in range(3):
+        arrive(g, max(1, 8 * g))
 
     q_hop(3, right, 1, 1).wait_recv()
     q_hop(1, left, 3, 4).wait_recv()
     q_hop(2, left, 1, 2).wait_recv()
     q_hop(2, right, 3, 5).wait_recv()
 
-    score[...] = jnp.zeros_like(score)
-
-    def score_step(j, carry):
-        score[...] += nt(p_all[:, cols(j)], q_all[:, cols(j)])
-        return carry
-
-    lax.fori_loop(0, D // CT, score_step, 0)
     qm, pm = q_all[:, D:], p_meta[...]
     l256 = iota((256, 128), 1)
-    permitted = nt(jnp.where(l256 < 16, pm.astype(F32), 0.0).astype(BF16), qm) > 0.5
+    reached = nt(jnp.where(l256 < 16, pm.astype(F32), 0.0).astype(BF16), qm)
+    live[...] = jnp.where(reached > 0.5, 1.0, 0.0)
     er, el = iota((8, 128), 0), iota((8, 128), 1)
     q_dig = nt(hot((er < 2) & (el == 16 + er)), qm)
     q_lo, q_hi = q_dig[0:1, :], q_dig[1:2, :]
     q_code = jnp.where(q_lo > 0.5, q_hi * 256.0 + q_lo, -2.0)
     p_lo = pm[:, 16:17].astype(F32)
-    p_dev = (shr(iota((256, 1), 0), 3) * NZ + z).astype(F32)
-    p_code = jnp.where(p_lo > 0.5, p_dev * 256.0 + p_lo, -1.0)
-    target = jnp.where(p_code == q_code, 1.0, 0.0)
-
-    s = score[...] * SCALE
+    slot = shr(iota((256, 1), 0), 3)
+    dx, dc = slot & 3, shr(slot, 4)
+    dy = (dx - shr(slot & 15, 2)) & 3
+    p_dev = (((x - dx) & 3) * 8 + ((y - dy) & 3) * 2 + ((c + dc) & 1)) * NZ + z
+    p_code = jnp.where(p_lo > 0.5, p_dev.astype(F32) * 256.0 + p_lo, -1.0)
+    target[...] = jnp.where(p_code == q_code, 1.0, 0.0)
+
+    score_rows(0, 192)
+    arrive(3, 24)
+    score_rows(192, 256)
+
+    s = score[...]
+    permitted = live[...] > 0.5
     top = jnp.max(jnp.where(permitted, s, FILL), axis=0, keepdims=True)
     total = jnp.sum(jnp.where(permitted, jnp.exp(s - top), 0.0), axis=0, keepdims=True)
     stat[0:1, :] = top
     stat[1:2, :] = total
     stat[2:8, :] = jnp.zeros((6, 256), F32)
     st_out = {dz: z_copy(stat, stat_in.at[dz - 1], zs_s, zs_r, dz) for dz in (1, 3, 2)}
-    for dz in (1, 3, 2):
+    for dz in (2, 1, 3):
         st_out[dz].start()
     for dz in (1, 3, 2):
         st_out[dz].wait_recv()
@@ -295,23 +315,25 @@
     row_total = sum(l * jnp.exp(m - row_top) for m, l in zip(tops, sums))
     prob = jnp.where(permitted, jnp.exp(s - row_top), 0.0)
     prob = prob / jnp.where(row_total > 0.0, row_total, 1.0)
-    gs = ((prob - target) * SCALE).astype(BF16)
-
-    dr, dc_ = iota((512, 256), 0), iota((512, 256), 1)
-    same = (shr(dr, 4) == shr(dc_, 3)) & ((dr & 7) == (dc_ & 7))
-    gs0 = nn(hot(same & ((dr & 8) == 0)), gs).astype(BF16)
-    gs1 = nn(hot(same & ((dr & 8) == 8)), gs).astype(BF16)
-
-    def ret_step(j, carry):
-        right = pl.ds(pl.multiple_of(PW + j * CT, CT), CT)
-        b_ret[:, cols(j)] = (nn(gs0, q_all[:, cols(j)]) + nn(gs1, q_all[:, right])).astype(BF16)
-        return carry
-
-    lax.fori_loop(0, PW // CT, ret_step, 0)
-    start_all(b_ret, b_back, br_s, br_r)
-    b_back[mine, :] = b_ret[mine, :]
-
-    gs_t = jnp.transpose(gs.astype(F32)).astype(BF16)
+    gs_f = (prob - target[...]) * SCALE
+    gs[...] = gs_f.astype(BF16)
+
+    dr, dq = iota((128, 64), 0), iota((128, 64), 1)
+    same = (shr(dr, 4) == shr(dq, 3)) & ((dr & 7) == (dq & 7))
+    dup = [hot(same & ((dr & 8) == 8 * h)) for h in range(2)]
+
+    def send_home(g):
+        part_gs = gs[g * 64 : (g + 1) * 64, :]
+        halves = [nn(dup[h], part_gs).astype(BF16) for h in range(2)]
+        for j in range(PW // CT):
+            acc = nn(halves[0], q_all[:, j * CT : (j + 1) * CT])
+            acc = acc + nn(halves[1], q_all[:, PW + j * CT : PW + (j + 1) * CT])
+            b_ret[g * 128 : (g + 1) * 128, j * CT : (j + 1) * CT] = acc.astype(BF16)
+        steps(max(1, 8 * g), 8 * (g + 1), lambda i: b_home(i, me).start())
+
+    send_home(0)
+
+    gs_t = jnp.transpose(gs_f).astype(BF16)
 
     def part_step(j, carry):
         part[:, cols(j)] = nn(gs_t, p_all[:, cols(j)]).astype(BF16)
@@ -333,6 +355,11 @@
     ]
     for copy in pt_out[:4]:
         copy.start()
+
+    for g in range(1, 4):
+        send_home(g)
+    b_back[mine, :] = b_ret[0:16, :]
+
     pt_out[0].wait_recv()
     up = part[block_rows(1), low].astype(F32) + relay_in[0].astype(F32)
     part[block_rows(1), low] = up.astype(BF16)
@@ -350,16 +377,15 @@
             acc = acc + part_in[i, :, ec].astype(F32)
         gq_stack[e * 64 : (e + 1) * 64, :] = acc.astype(BF16)
     a_ret[...] = tn(sel_q[...], gq_stack[...]).astype(BF16)
-    start_all(a_ret, a_back, ar_s, ar_r)
-    a_back[mine, :] = a_ret[mine, :]
-
-    await_recv(b_ret, b_back, br_s, br_r)
-    await_recv(a_ret, a_back, ar_s, ar_r)
-
-    await_send(a_send, a_recv, as_s, as_r)
-    await_send(b_send, b_recv, bs_s, bs_r)
-    await_send(b_ret, b_back, br_s, br_r)
-    await_send(a_ret, a_back, ar_s, ar_r)
+    steps(1, NB, lambda i: a_home(i, me).start())
+    a_back[mine, :] = a_ret[0:16, :]
+    steps(1, NB, lambda i: b_home(i, partner(i)).wait_recv())
+    steps(1, NB, lambda i: a_home(i, partner(i)).wait_recv())
+
+    steps(1, NB, lambda i: a_out(i).wait_send())
+    steps(1, NB, lambda i: b_out(i).wait_send())
+    steps(1, NB, lambda i: b_home(i, me).wait_send())
+    steps(1, NB, lambda i: a_home(i, me).wait_send())
     for copy in q_out + pt_out:
         copy.wait_send()
     for dz in (1, 3, 2):
@@ -411,7 +437,9 @@
             vm((16, 256), I32), vm((128, 256), BF16),
             vm((1, 32), I32), vm((1, 32), I32), vm((1, 128), I32),
             vm((256, 128), BF16),
-            vm((256, D + 128), BF16), vm((256, D), BF16), vm((256, 256), F32),
+            vm((256, D + 128), BF16), vm((256, D), BF16),
+            vm((256, 256), F32), vm((256, 256), F32), vm((256, 256), F32),
+            vm((256, 256), BF16),
             vm((256, D), BF16), vm((2, 64, PW), BF16), vm((2, 64, D), BF16),
             vm((8, 256), F32), vm((3, 8, 256), F32),
         ]

time: 90.6 us -> 86.9 us (0.959)
  Pallas kernels: 89.8 us -> 86.2 us
    pallas_call x1, Pallas kernels: 88.2 us -> 84.5 us  [per_device(): pl.pallas_call(kernel, out_shape=(pltpu.VMEM((512, QW), BF16), pltpu.VMEM...]
where the time goes in v3:
time: 86.9 us; the launch traced here: 86.8 us
  Pallas kernels  86.2 us (99%)
    pallas_call x1, Pallas kernels, per_device(): pl.pallas_call(kernel, out_shape=(pltpu.VMEM((512, QW), BF16), pltpu.VMEM...  84.5 us

profile of v3, /device:TPU:1, one launch (start us, length us, event | category | flops | bytes accessed | tf_op | source)
XLA Modules:
  0.0 86.8 jit_solution(4656283064383153927)
XLA Ops:
  0.6 84.5 %contrastive.1 = (bf16[512,512]{1,0:T(8,128)(2,1)S(1)}, bf16[512,2048]{1,0:T(8,128)(2,1)S(1)}, bf16[512,256]{1,0:T(8,128)(2,1)S(1)}, bf16[512,256]{1,0:T(8,128)(2,1)S(1)}) custom-call(bf16[32,4096]{1,0:T(8,128)(2,1)} %q_hbm.1, bf16[128,4096]{1,0:T(8,128)(2,1)} %p_hbm.1, s32[1,32]{1,0:T(1,128)} %bitcast.5, s32[1,32]{1,0:T(1,128)} %bitcast.6, ...), custom_call_target="tpu_custom_call" | custom-call | tf_op jit(solution)/shard_map/contrastive/pallas_call | solution.py:421
  85.1 1.7 %unpack.1 = (bf16[32,4096]{1,0:T(8,128)(2,1)}, bf16[128,4096]{1,0:T(8,128)(2,1)}) custom-call(bf16[512,512]{1,0:T(8,128)(2,1)S(1)} %get-tuple-element.6.a_back, bf16[512,2048]{1,0:T(8,128)(2,1)S(1)} %get-tuple-element.7.b_back, bf16[512,256]{1,0:T(8,128)(2,1)S(1)} %get-tuple-element.8.g_q, bf16[512,256]{1,0:T(8,128)(2,1)S(1)} %get-tuple-element.9.g_p), custom_call_target="tpu_custom_call" | custom-call | tf_op jit(solution)/shard_map/unpack/pallas_call | solution.py:463

commit v4 on v3

--- a/solution.py
+++ b/solution.py
@@ -51,23 +51,32 @@
     return pl.ds(pl.multiple_of(i * 16, 16), 16)
 
 
+def offset(i):
+    j = i % 16
+    dx = j % 4
+    return dx, (dx + 4 - j // 4) % 4, i // 16
+
+
+def hops(i):
+    dx, dy, _ = offset(i)
+    return min(dx, 4 - dx) + min(dy, 4 - dy)
+
+
+FAR_FIRST = sorted(range(1, NB), key=hops, reverse=True)
+
+
 def kernel(
     q_hbm, p_hbm, qc_hbm, pos_hbm, pc_hbm, allowed_hbm,
     a_back, b_back, g_q, g_p,
     a_send, a_recv, b_send, b_recv, a_ret, b_ret,
     q_stack, p_stack, gq_stack, sel_q, allow_int, allow_buf, qc_buf, pos_buf, pc_buf, p_meta,
-    q_all, p_all, score, live, target, gs, part, relay_in, part_in, stat, stat_in,
+    q_all, q_t, p_all, score, live, target, gs, part, relay_in, part_in, stat, stat_in,
     as_s, as_r, bs_s, bs_r, ar_s, ar_r, br_s, br_r, zq_s, zq_r, zs_s, zs_r, zg_s, zg_r, in_sem,
 ):
     me = lax.axis_index("pb")
     z = lax.axis_index("pa")
     x, y, c = me // 8, (me // 2) % 4, me % 2
 
-    def offset(i):
-        j = i % 16
-        dx = j % 4
-        return dx, (dx + 4 - j // 4) % 4, i // 16
-
     def partner(i):
         dx, dy, dc = offset(i)
         return ((x + dx) % 4) * 8 + ((y + dy) % 4) * 2 + (c + dc) % 2
@@ -75,6 +84,12 @@
     def origin(i):
         dx, dy, dc = offset(i)
         return ((x + 4 - dx) % 4) * 8 + ((y + 4 - dy) % 4) * 2 + (c + dc) % 2
+
+    barrier = pltpu.get_barrier_semaphore()
+    for i in FAR_FIRST:
+        pl.semaphore_signal(barrier, inc=1, device_id=(partner(i), z), device_id_type=MESH)
+    for dz in (2, 1, 3):
+        pl.semaphore_signal(barrier, inc=1, device_id=(me, (z + dz) % NZ), device_id_type=MESH)
 
     loads = [
         pltpu.make_async_copy(qc_hbm, qc_buf, in_sem.at[0]),
@@ -101,16 +116,6 @@
     for load in loads:
         load.start()
 
-    barrier = pltpu.get_barrier_semaphore()
-
-    def greet(i, carry):
-        pl.semaphore_signal(barrier, inc=1, device_id=(partner(i), z), device_id_type=MESH)
-        return carry
-
-    lax.fori_loop(1, NB, greet, 0)
-    for dz in range(1, NZ):
-        pl.semaphore_signal(barrier, inc=1, device_id=(me, (z + dz) % NZ), device_id_type=MESH)
-
     for load in loads[:4]:
         load.wait()
     qc_row, pos_row, pc_row = qc_buf[...], pos_buf[...], pc_buf[...]
@@ -264,10 +269,16 @@
                 p_all[g * 64 : (g + 1) * 64, columns] = nn(sel_u[h], got).astype(BF16)
 
     def score_rows(lo, hi):
-        acc = nt(p_all[lo:hi, 0:CT], q_all[:, 0:CT])
+        acc = nn(p_all[lo:hi, 0:CT], q_t[0:CT, :])
         for j in range(1, D // CT):
-            acc = acc + nt(p_all[lo:hi, j * CT : (j + 1) * CT], q_all[:, j * CT : (j + 1) * CT])
-        score[lo:hi, :] = acc * SCALE
+            acc = acc + nn(p_all[lo:hi, j * CT : (j + 1) * CT], q_t[j * CT : (j + 1) * CT, :])
+        return acc * SCALE
+
+    def row_stats(s, lo, hi):
+        permitted = live[lo:hi, :] > 0.5
+        top = jnp.max(jnp.where(permitted, s, FILL), axis=0, keepdims=True)
+        e = jnp.where(permitted, jnp.exp(s - top), 0.0)
+        return top, jnp.sum(e, axis=0, keepdims=True), e
 
     for g in range(3):
         arrive(g, max(1, 8 * g))
@@ -291,32 +302,37 @@
     dy = (dx - shr(slot & 15, 2)) & 3
     p_dev = (((x - dx) & 3) * 8 + ((y - dy) & 3) * 2 + ((c + dc) & 1)) * NZ + z
     p_code = jnp.where(p_lo > 0.5, p_dev.astype(F32) * 256.0 + p_lo, -1.0)
-    target[...] = jnp.where(p_code == q_code, 1.0, 0.0)
-
-    score_rows(0, 192)
+    target[...] = jnp.where(p_code == q_code, SCALE, 0.0)
+
+    def turn(j, carry):
+        q_t[cols(j), :] = jnp.transpose(q_all[:, cols(j)].astype(F32)).astype(BF16)
+        return carry
+
+    lax.fori_loop(0, D // CT, turn, 0)
+    top_a, total_a, e_a = row_stats(score_rows(0, 192), 0, 192)
+    score[0:192, :] = e_a
     arrive(3, 24)
-    score_rows(192, 256)
-
-    s = score[...]
-    permitted = live[...] > 0.5
-    top = jnp.max(jnp.where(permitted, s, FILL), axis=0, keepdims=True)
-    total = jnp.sum(jnp.where(permitted, jnp.exp(s - top), 0.0), axis=0, keepdims=True)
+    top_b, total_b, e_b = row_stats(score_rows(192, 256), 192, 256)
+    top = jnp.maximum(top_a, top_b)
+    fix_a, fix_b = jnp.exp(top_a - top), jnp.exp(top_b - top)
+    total = total_a * fix_a + total_b * fix_b
+
     stat[0:1, :] = top
     stat[1:2, :] = total
     stat[2:8, :] = jnp.zeros((6, 256), F32)
     st_out = {dz: z_copy(stat, stat_in.at[dz - 1], zs_s, zs_r, dz) for dz in (1, 3, 2)}
     for dz in (2, 1, 3):
         st_out[dz].start()
+    score[192:256, :] = e_b
     for dz in (1, 3, 2):
         st_out[dz].wait_recv()
     tops = [top] + [stat_in[i, 0:1, :] for i in range(3)]
     sums = [total] + [stat_in[i, 1:2, :] for i in range(3)]
     row_top = jnp.maximum(jnp.maximum(tops[0], tops[1]), jnp.maximum(tops[2], tops[3]))
     row_total = sum(l * jnp.exp(m - row_top) for m, l in zip(tops, sums))
-    prob = jnp.where(permitted, jnp.exp(s - row_top), 0.0)
-    prob = prob / jnp.where(row_total > 0.0, row_total, 1.0)
-    gs_f = (prob - target[...]) * SCALE
-    gs[...] = gs_f.astype(BF16)
+    share = SCALE * jnp.exp(top - row_top) / jnp.where(row_total > 0.0, row_total, 1.0)
+    gs[0:192, :] = (score[0:192, :] * (share * fix_a) - target[0:192, :]).astype(BF16)
+    gs[192:256, :] = (score[192:256, :] * (share * fix_b) - target[192:256, :]).astype(BF16)
 
     dr, dq = iota((128, 64), 0), iota((128, 64), 1)
     same = (shr(dr, 4) == shr(dq, 3)) & ((dr & 7) == (dq & 7))
@@ -333,7 +349,7 @@
 
     send_home(0)
 
-    gs_t = jnp.transpose(gs_f).astype(BF16)
+    gs_t = jnp.transpose(gs[...].astype(F32)).astype(BF16)
 
     def part_step(j, carry):
         part[:, cols(j)] = nn(gs_t, p_all[:, cols(j)]).astype(BF16)
@@ -437,7 +453,7 @@
             vm((16, 256), I32), vm((128, 256), BF16),
             vm((1, 32), I32), vm((1, 32), I32), vm((1, 128), I32),
             vm((256, 128), BF16),
-            vm((256, D + 128), BF16), vm((256, D), BF16),
+            vm((256, D + 128), BF16), vm((D, 256), BF16), vm((256, D), BF16),
             vm((256, 256), F32), vm((256, 256), F32), vm((256, 256), F32),
             vm((256, 256), BF16),
             vm((256, D), BF16), vm((2, 64, PW), BF16), vm((2, 64, D), BF16),

time: 86.9 us -> 84.5 us (0.972)
  Pallas kernels: 86.2 us -> 83.7 us
    pallas_call x1, Pallas kernels: 84.5 us -> 82 us  [per_device(): pl.pallas_call(kernel, out_shape=(pltpu.VMEM((512, QW), BF16), pltpu.VMEM...]
where the time goes in v4:
time: 84.5 us; the launch traced here: 84.4 us
  Pallas kernels  83.7 us (99%)
    pallas_call x1, Pallas kernels, per_device(): pl.pallas_call(kernel, out_shape=(pltpu.VMEM((512, QW), BF16), pltpu.VMEM...  82 us

profile of v4, /device:TPU:1, one launch (start us, length us, event | category | flops | bytes accessed | tf_op | source)
XLA Modules:
  0.0 84.4 jit_solution(16428460858346648054)
XLA Ops:
  0.6 82.0 %contrastive.1 = (bf16[512,512]{1,0:T(8,128)(2,1)S(1)}, bf16[512,2048]{1,0:T(8,128)(2,1)S(1)}, bf16[512,256]{1,0:T(8,128)(2,1)S(1)}, bf16[512,256]{1,0:T(8,128)(2,1)S(1)}) custom-call(bf16[32,4096]{1,0:T(8,128)(2,1)} %q_hbm.1, bf16[128,4096]{1,0:T(8,128)(2,1)} %p_hbm.1, s32[1,32]{1,0:T(1,128)} %bitcast.5, s32[1,32]{1,0:T(1,128)} %bitcast.6, ...), custom_call_target="tpu_custom_call" | custom-call | tf_op jit(solution)/shard_map/contrastive/pallas_call | solution.py:437
  82.7 1.7 %unpack.1 = (bf16[32,4096]{1,0:T(8,128)(2,1)}, bf16[128,4096]{1,0:T(8,128)(2,1)}) custom-call(bf16[512,512]{1,0:T(8,128)(2,1)S(1)} %get-tuple-element.6.a_back, bf16[512,2048]{1,0:T(8,128)(2,1)S(1)} %get-tuple-element.7.b_back, bf16[512,256]{1,0:T(8,128)(2,1)S(1)} %get-tuple-element.8.g_q, bf16[512,256]{1,0:T(8,128)(2,1)S(1)} %get-tuple-element.9.g_p), custom_call_target="tpu_custom_call" | custom-call | tf_op jit(solution)/shard_map/unpack/pallas_call | solution.py:479

commit v5 on v4

--- a/solution.py
+++ b/solution.py
@@ -67,8 +67,8 @@
 
 def kernel(
     q_hbm, p_hbm, qc_hbm, pos_hbm, pc_hbm, allowed_hbm,
-    a_back, b_back, g_q, g_p,
-    a_send, a_recv, b_send, b_recv, a_ret, b_ret,
+    a_back, p_grad, g_q,
+    b_back, g_p, a_send, a_recv, b_send, b_recv, a_ret, b_ret,
     q_stack, p_stack, gq_stack, sel_q, allow_int, allow_buf, qc_buf, pos_buf, pc_buf, p_meta,
     q_all, q_t, p_all, score, live, target, gs, part, relay_in, part_in, stat, stat_in,
     as_s, as_r, bs_s, bs_r, ar_s, ar_r, br_s, br_r, zq_s, zq_r, zs_s, zs_r, zg_s, zg_r, in_sem,
@@ -229,33 +229,48 @@
     hr, hc = iota((256, 512), 0), iota((256, 512), 1)
     half = (shr(hr, 3) == shr(hc, 4)) & ((hr & 7) == (hc & 7))
     sel_m = hot(half & ((hc & 8) == 0))
-    nr, nc = iota((64, 512), 0), iota((64, 512), 1)
+    wr, wc = iota((128, 128), 0), iota((128, 128), 1)
+    sel_w = hot((shr(wr, 4) == (wc & 7)) & ((wr & 15) == shr(wc, 3)))
+    nr, nc = iota((16, 128), 0), iota((16, 128), 1)
     sel_n = hot((shr(nr, 1) == shr(nc, 4)) & ((nc & 15) == 8 + (nr & 1)))
 
-    steps(1, NB, lambda i: a_out(i).wait_recv())
-    zrows = pl.ds(pl.multiple_of(z * 64, 64), 64)
-    whole = nn(sel_q[...], a_recv[:, 0:QW]).astype(BF16)
-    for e in range(8):
-        q_all[zrows, e * QW : (e + 1) * QW] = whole[e * 64 : (e + 1) * 64, :]
-    q_all[zrows, D:] = nn(sel_n, a_recv[:, QW:]).astype(BF16)
     left, right = slice(0, PW), slice(PW, D + 128)
 
-    def q_hop(dz_block, columns, dz, k):
-        piece = q_all.at[block_rows(dz_block), columns]
-        return z_copy(piece, piece, zq_s, zq_r, dz, k)
-
-    q_out = [
-        q_hop(0, left, 1, 0), q_hop(0, right, 3, 3), q_hop(0, right, 1, 1), q_hop(0, left, 3, 4),
-        q_hop(3, left, 1, 2), q_hop(1, right, 3, 5),
-    ]
-    for copy in q_out[:4]:
+    def group_rows(dz, g):
+        return pl.ds(pl.multiple_of(((z + dz) % NZ) * 64 + g * 16, 16), 16)
+
+    def q_hop(dz_block, columns, dz, k, g):
+        piece = q_all.at[group_rows(dz_block, g), columns]
+        return z_copy(piece, piece, zq_s, zq_r, dz, g * 6 + k)
+
+    q_out = []
+
+    def send_on(copy):
         copy.start()
+        q_out.append(copy)
+
+    def relay(g):
+        q_hop(3, left, 1, 0, g).wait_recv()
+        send_on(q_hop(3, left, 1, 2, g))
+        q_hop(1, right, 3, 3, g).wait_recv()
+        send_on(q_hop(1, right, 3, 5, g))
+
+    for g in range(4):
+        steps(max(1, 8 * g), 8 * (g + 1), lambda i: a_out(i).wait_recv())
+        come = slice(128 * g, 128 * (g + 1))
+        whole = nn(sel_w, a_recv[come, 0:QW]).astype(BF16)
+        rows = group_rows(0, g)
+        for e in range(8):
+            q_all[rows, e * QW : (e + 1) * QW] = whole[e * 16 : (e + 1) * 16, :]
+        q_all[rows, D:] = nn(sel_n, a_recv[come, QW:]).astype(BF16)
+        send_on(q_hop(0, left, 1, 0, g))
+        send_on(q_hop(0, right, 3, 3, g))
+        send_on(q_hop(0, right, 1, 1, g))
+        send_on(q_hop(0, left, 3, 4, g))
+        if g:
+            relay(g - 1)
+    relay(3)
     p_meta[...] = nn(sel_m, a_recv[:, QW:]).astype(BF16)
-    q_hop(3, left, 1, 0).wait_recv()
-    q_out[4].start()
-    q_hop(1, right, 3, 3).wait_recv()
-    q_out[5].start()
-
     ur, uc = iota((64, 128), 0), iota((64, 128), 1)
     pair = (shr(ur, 3) == shr(uc, 4)) & ((ur & 7) == (uc & 7))
     sel_u = [hot(pair & ((uc & 8) == 8 * h)) for h in range(2)]
@@ -283,10 +298,11 @@
     for g in range(3):
         arrive(g, max(1, 8 * g))
 
-    q_hop(3, right, 1, 1).wait_recv()
-    q_hop(1, left, 3, 4).wait_recv()
-    q_hop(2, left, 1, 2).wait_recv()
-    q_hop(2, right, 3, 5).wait_recv()
+    for g in range(4):
+        q_hop(3, right, 1, 1, g).wait_recv()
+        q_hop(1, left, 3, 4, g).wait_recv()
+        q_hop(2, left, 1, 2, g).wait_recv()
+        q_hop(2, right, 3, 5, g).wait_recv()
 
     qm, pm = q_all[:, D:], p_meta[...]
     l256 = iota((256, 128), 1)
@@ -388,7 +404,7 @@
         copy.wait_recv()
     for e in range(8):
         ec = slice(e * QW, (e + 1) * QW)
-        acc = part[zrows, ec].astype(F32)
+        acc = part[block_rows(0), ec].astype(F32)
         for i in range(2):
             acc = acc + part_in[i, :, ec].astype(F32)
         gq_stack[e * 64 : (e + 1) * 64, :] = acc.astype(BF16)
@@ -396,6 +412,11 @@
     steps(1, NB, lambda i: a_home(i, me).start())
     a_back[mine, :] = a_ret[0:16, :]
     steps(1, NB, lambda i: b_home(i, partner(i)).wait_recv())
+    for j in range(PW // CT):
+        got = tn(g_p[...], b_back[:, j * CT : (j + 1) * CT]).astype(BF16)
+        for h in range(2):
+            columns = slice(h * PW + j * CT, h * PW + (j + 1) * CT)
+            p_grad[:, columns] = got[h * 128 : (h + 1) * 128, :]
     steps(1, NB, lambda i: a_home(i, partner(i)).wait_recv())
 
     steps(1, NB, lambda i: a_out(i).wait_send())
@@ -408,25 +429,21 @@
         st_out[dz].wait_send()
 
 
-def unpack(a_back, b_back, g_q, g_p, outq_hbm, outp_hbm, q_buf, p_buf, sem):
+def unpack(a_back, p_grad, g_q, outq_hbm, outp_hbm, q_buf, sem):
     copies = []
-    for j in range(PW // CT):
-        got = tn(g_p[...], b_back[:, j * CT : (j + 1) * CT]).astype(BF16)
-        for h in range(2):
-            columns = slice(h * PW + j * CT, h * PW + (j + 1) * CT)
-            p_buf[:, columns] = got[h * 128 : (h + 1) * 128, :]
-            copy = pltpu.make_async_copy(
-                p_buf.at[:, columns], outp_hbm.at[:, columns], sem.at[2 * j + h]
-            )
-            copy.start()
-            copies.append(copy)
+    for h in range(8):
+        rows = slice(h * 16, (h + 1) * 16)
+        copies.append(pltpu.make_async_copy(p_grad.at[rows, :], outp_hbm.at[rows, :], sem.at[h]))
+        copies[-1].start()
     back = tn(g_q[...], a_back[...]).astype(BF16)
     for e in range(8):
         q_buf[:, e * QW : (e + 1) * QW] = back[e * 32 : (e + 1) * 32, :]
-    copy = pltpu.make_async_copy(q_buf, outq_hbm, sem.at[8])
-    copy.start()
-    for c in copies + [copy]:
-        c.wait()
+    for h in range(2):
+        rows = slice(h * 16, (h + 1) * 16)
+        copies.append(pltpu.make_async_copy(q_buf.at[rows, :], outq_hbm.at[rows, :], sem.at[8 + h]))
+        copies[-1].start()
+    for copy in copies:
+        copy.wait()
 
 
 def per_device(queries, passages, query_cluster, passage_cluster, allowed, positive):
@@ -438,13 +455,13 @@
         kernel,
         out_shape=(
             pltpu.VMEM((512, QW), BF16),
-            pltpu.VMEM((512, PW), BF16),
-            pltpu.VMEM((512, 256), BF16),
+            pltpu.VMEM((128, D), BF16),
             pltpu.VMEM((512, 256), BF16),
         ),
         in_specs=[pl.BlockSpec(memory_space=pltpu.HBM)] * 6,
-        out_specs=(res,) * 4,
+        out_specs=(res,) * 3,
         scratch_shapes=[
+            vm((512, PW), BF16), vm((512, 256), BF16),
             vm((512, QW + 128), BF16), vm((512, QW + 128), BF16),
             vm((512, PW), BF16), vm((512, PW), BF16),
             vm((512, QW), BF16), vm((512, PW), BF16),
@@ -460,7 +477,7 @@
             vm((8, 256), F32), vm((3, 8, 256), F32),
         ]
         + [dma((NB,))] * 8
-        + [dma((6,))] * 2
+        + [dma((24,))] * 2
         + [dma((3,))] * 2
         + [dma((6,))] * 2
         + [dma((14,))],
@@ -482,9 +499,9 @@
             jax.ShapeDtypeStruct(queries.shape, BF16),
             jax.ShapeDtypeStruct(passages.shape, BF16),
         ),
-        in_specs=[res] * 4,
+        in_specs=[res] * 3,
         out_specs=(hbm, hbm),
-        scratch_shapes=[vm((32, D), BF16), vm((128, D), BF16), dma((9,))],
+        scratch_shapes=[vm((32, D), BF16), dma((10,))],
         compiler_params=pltpu.CompilerParams(vmem_limit_bytes=16 * 1024 * 1024),
         name="unpack",
     )(*landed)

time: 84.5 us -> 83.8 us (level)
  no operation moved by 1% of the time
where the time goes in v5:
time: 83.8 us; the launch traced here: 83.7 us
  Pallas kernels  83.1 us (99%)
    pallas_call x1, Pallas kernels, per_device(): pl.pallas_call(kernel, out_shape=(pltpu.VMEM((512, QW), BF16), pltpu.VMEM...  81.9 us

profile of v5, /device:TPU:1, one launch (start us, length us, event | category | flops | bytes accessed | tf_op | source)
XLA Modules:
  0.0 83.7 jit_solution(17089569238712956307)
XLA Ops:
  0.6 81.9 %contrastive.1 = (bf16[512,512]{1,0:T(8,128)(2,1)S(1)}, bf16[128,4096]{1,0:T(8,128)(2,1)S(1)}, bf16[512,256]{1,0:T(8,128)(2,1)S(1)}) custom-call(bf16[32,4096]{1,0:T(8,128)(2,1)} %q_hbm.1, bf16[128,4096]{1,0:T(8,128)(2,1)} %p_hbm.1, s32[1,32]{1,0:T(1,128)} %bitcast.5, s32[1,32]{1,0:T(1,128)} %bitcast.6, s32[1,128]{1,0:T(1,128)} %bitcast.7, s32[16,256]{1,0:T(8,128)} %bitcast.4), custom_call_target="tpu_custom_call" | custom-call | tf_op jit(solution)/shard_map/contrastive/pallas_call | solution.py:454
  82.6 1.1 %unpack.1 = (bf16[32,4096]{1,0:T(8,128)(2,1)}, bf16[128,4096]{1,0:T(8,128)(2,1)}) custom-call(bf16[512,512]{1,0:T(8,128)(2,1)S(1)} %get-tuple-element.5.a_back, bf16[128,4096]{1,0:T(8,128)(2,1)S(1)} %get-tuple-element.6.p_grad, bf16[512,256]{1,0:T(8,128)(2,1)S(1)} %get-tuple-element.7.g_q), custom_call_target="tpu_custom_call" | custom-call | tf_op jit(solution)/shard_map/unpack/pallas_call | solution.py:496

commit v6 on v5

--- a/solution.py
+++ b/solution.py
@@ -69,9 +69,9 @@
     q_hbm, p_hbm, qc_hbm, pos_hbm, pc_hbm, allowed_hbm,
     a_back, p_grad, g_q,
     b_back, g_p, a_send, a_recv, b_send, b_recv, a_ret, b_ret,
-    q_stack, p_stack, gq_stack, sel_q, allow_int, allow_buf, qc_buf, pos_buf, pc_buf, p_meta,
+    q_stack, p_stack, gq_stack, sel_q, allow_int, allow_buf, qc_buf, pos_buf, pc_buf, m_send, m_recv, m_flat,
     q_all, q_t, p_all, score, live, target, gs, part, relay_in, part_in, stat, stat_in,
-    as_s, as_r, bs_s, bs_r, ar_s, ar_r, br_s, br_r, zq_s, zq_r, zs_s, zs_r, zg_s, zg_r, in_sem,
+    as_s, as_r, ms_s, ms_r, bs_s, bs_r, ar_s, ar_r, br_s, br_r, zq_s, zq_r, zs_s, zs_r, zg_s, zg_r, in_sem,
 ):
     me = lax.axis_index("pb")
     z = lax.axis_index("pa")
@@ -143,22 +143,33 @@
     g_p[:, 128:256] = hot(here & ((half_r & 8) == 8))
 
     allow_buf[...] = jnp.zeros_like(allow_buf)
-    allow_buf[0:16, :] = allow_int[...].astype(F32).astype(BF16)
-    l256c = iota((32, 256), 1)
-    reach = nt(hot(l256c == qc_col), allow_buf[...])
+    table = allow_int[...].astype(F32).astype(BF16)
+    allow_buf[16:32, :] = table
+    allow_buf[32:48, :] = table
+    reach = nt(hot(iota((32, 256), 1) == qc_col), allow_buf[...])
+    q_slot_col = jnp.sum(jnp.where(lane32 == sub32, q_slot, 0), axis=1, keepdims=True)
+    p_slot_col = jnp.sum(jnp.where(lane128 == sub128, p_slot, 0), axis=1, keepdims=True)
     l32 = iota((32, 128), 1)
-    q_num = jnp.where(l32 < 16, reach, 0.0)
-    q_num = jnp.where(l32 == 16, (pos_col & 127).astype(F32) + 1.0, q_num)
-    q_num = jnp.where(l32 == 17, shr(pos_col, 7).astype(F32), q_num).astype(BF16)
-    p_num = jnp.where((lane128 < 16) & ((pc_col & 15) == lane128), 1.0, 0.0)
-    p_num = jnp.where(lane128 == 16, sub128.astype(F32) + 1.0, p_num).astype(BF16)
-    mr_p, mr_q = iota((512, 128), 0), iota((512, 32), 0)
-    gm_p = hot((p_slot == shr(mr_p, 4) * 8 + (mr_p & 15)) & ((mr_p & 15) < 8))
-    gm_q = hot((q_slot == shr(mr_q, 4) * 2 + (mr_q & 15) - 8) & (shr(mr_q & 15, 1) == 4))
-    a_send[:, QW:] = (nn(gm_p, p_num) + nn(gm_q, q_num)).astype(BF16)
+    second = q_slot_col & 1
+    q_num = jnp.where(shr(l32, 4) == 1 + second, reach, 0.0)
+    q_num = jnp.where(l32 == 48 + second, (pos_col & 127).astype(F32) + 1.0, q_num)
+    q_num = jnp.where(l32 == 50 + second, shr(pos_col, 7).astype(F32), q_num).astype(BF16)
+    kth = p_slot_col & 7
+    p_num = jnp.where(lane128 == kth, sub128.astype(F32) + 1.0, 0.0)
+    p_num = jnp.where(lane128 == 8 + kth, (pc_col & 15).astype(F32), p_num).astype(BF16)
+    to_q = hot(shr(q_slot, 1) == iota((32, 32), 0))
+    to_p = hot(shr(p_slot, 3) == iota((32, 128), 0))
+    m_flat[...] = nn(to_p, p_num) + nn(to_q, q_num)
+
+    def spread_rows(i, carry):
+        m_send[i] = m_flat[pl.ds(i, 1), :]
+        return carry
+
+    lax.fori_loop(0, NB, spread_rows, 0)
+    m_flat[...] = jnp.zeros_like(m_flat)
     for load in loads[4:12]:
         load.wait()
-    a_send[:, 0:QW] = nn(g_q[...], q_stack[...]).astype(BF16)
+    a_send[...] = nn(g_q[...], q_stack[...]).astype(BF16)
 
     pl.semaphore_wait(barrier, NB - 1 + NZ - 1)
 
@@ -173,6 +184,17 @@
             device_id_type=MESH,
         )
 
+    def m_out(i):
+        d = partner(i)
+        return pltpu.make_async_remote_copy(
+            src_ref=m_send.at[d],
+            dst_ref=m_recv.at[i],
+            send_sem=ms_s.at[i],
+            recv_sem=ms_r.at[i],
+            device_id=(d, z),
+            device_id_type=MESH,
+        )
+
     def back_copy(src, dst, send, recv, i, place):
         return pltpu.make_async_remote_copy(
             src_ref=src.at[rows16(i), :],
@@ -210,8 +232,13 @@
         return pl.ds(pl.multiple_of(((z + dz) % NZ) * 64, 64), 64)
 
     mine = rows16(me)
-    steps(1, NB, lambda i: a_out(i).start())
+    def send_queries(i):
+        a_out(i).start()
+        m_out(i).start()
+
+    steps(1, NB, send_queries)
     a_recv[0:16, :] = a_send[mine, :]
+    m_recv[0] = m_send[me]
 
     for load in loads[12:]:
         load.wait()
@@ -226,13 +253,18 @@
 
     sr, sc = iota((512, 512), 0), iota((512, 512), 1)
     sel_q[...] = hot((shr(sr, 6) == (sc & 7)) & ((sr & 63) == shr(sc, 3)))
-    hr, hc = iota((256, 512), 0), iota((256, 512), 1)
-    half = (shr(hr, 3) == shr(hc, 4)) & ((hr & 7) == (hc & 7))
-    sel_m = hot(half & ((hc & 8) == 0))
     wr, wc = iota((128, 128), 0), iota((128, 128), 1)
     sel_w = hot((shr(wr, 4) == (wc & 7)) & ((wr & 15) == shr(wc, 3)))
-    nr, nc = iota((16, 128), 0), iota((16, 128), 1)
-    sel_n = hot((shr(nr, 1) == shr(nc, 4)) & ((nc & 15) == 8 + (nr & 1)))
+    fr, fc = iota((128, 128), 0), iota((128, 128), 1)
+    pick = [
+        hot(
+            ((fr == 16 + 16 * r + fc) & (fc < 16))
+            | ((fr == 48 + r) & (fc == 16))
+            | ((fr == 50 + r) & (fc == 17))
+        )
+        for r in range(2)
+    ]
+    first = (iota((16, 128), 0) & 1) == 0
 
     left, right = slice(0, PW), slice(PW, D + 128)
 
@@ -256,13 +288,23 @@
         send_on(q_hop(1, right, 3, 5, g))
 
     for g in range(4):
-        steps(max(1, 8 * g), 8 * (g + 1), lambda i: a_out(i).wait_recv())
+        def take(i):
+            m_flat[pl.ds(i, 1), :] = m_recv[i]
+
+        def await_queries(i):
+            a_out(i).wait_recv()
+            m_out(i).wait_recv()
+
+        steps(max(1, 8 * g), 8 * (g + 1), await_queries)
+        steps(8 * g, 8 * (g + 1), take)
         come = slice(128 * g, 128 * (g + 1))
-        whole = nn(sel_w, a_recv[come, 0:QW]).astype(BF16)
+        whole = nn(sel_w, a_recv[come, :]).astype(BF16)
         rows = group_rows(0, g)
         for e in range(8):
             q_all[rows, e * QW : (e + 1) * QW] = whole[e * 16 : (e + 1) * 16, :]
-        q_all[rows, D:] = nn(sel_n, a_recv[come, QW:]).astype(BF16)
+        twice = hot(iota((16, 32), 1) == 8 * g + shr(iota((16, 32), 0), 1))
+        nums = nn(twice, m_flat[...].astype(BF16)).astype(BF16)
+        q_all[rows, D:] = jnp.where(first, nn(nums, pick[0]), nn(nums, pick[1])).astype(BF16)
         send_on(q_hop(0, left, 1, 0, g))
         send_on(q_hop(0, right, 3, 3, g))
         send_on(q_hop(0, right, 1, 1, g))
@@ -270,7 +312,6 @@
         if g:
             relay(g - 1)
     relay(3)
-    p_meta[...] = nn(sel_m, a_recv[:, QW:]).astype(BF16)
     ur, uc = iota((64, 128), 0), iota((64, 128), 1)
     pair = (shr(ur, 3) == shr(uc, 4)) & ((ur & 7) == (uc & 7))
     sel_u = [hot(pair & ((uc & 8) == 8 * h)) for h in range(2)]
@@ -304,15 +345,18 @@
         q_hop(2, left, 1, 2, g).wait_recv()
         q_hop(2, right, 3, 5, g).wait_recv()
 
-    qm, pm = q_all[:, D:], p_meta[...]
-    l256 = iota((256, 128), 1)
-    reached = nt(jnp.where(l256 < 16, pm.astype(F32), 0.0).astype(BF16), qm)
+    qm = q_all[:, D:]
+    eightfold = hot(iota((256, 32), 1) == shr(iota((256, 32), 0), 3))
+    p_nums = nn(eightfold, m_flat[...].astype(BF16))
+    l256, k256 = iota((256, 128), 1), iota((256, 128), 0) & 7
+    p_lo = jnp.sum(jnp.where(l256 == k256, p_nums, 0.0), axis=1, keepdims=True)
+    p_cl = jnp.sum(jnp.where(l256 == 8 + k256, p_nums, 0.0), axis=1, keepdims=True)
+    reached = nt(hot((l256.astype(F32) == p_cl) & (p_lo > 0.5)), qm)
     live[...] = jnp.where(reached > 0.5, 1.0, 0.0)
     er, el = iota((8, 128), 0), iota((8, 128), 1)
     q_dig = nt(hot((er < 2) & (el == 16 + er)), qm)
     q_lo, q_hi = q_dig[0:1, :], q_dig[1:2, :]
     q_code = jnp.where(q_lo > 0.5, q_hi * 256.0 + q_lo, -2.0)
-    p_lo = pm[:, 16:17].astype(F32)
     slot = shr(iota((256, 1), 0), 3)
     dx, dc = slot & 3, shr(slot, 4)
     dy = (dx - shr(slot & 15, 2)) & 3
@@ -420,6 +464,7 @@
     steps(1, NB, lambda i: a_home(i, partner(i)).wait_recv())
 
     steps(1, NB, lambda i: a_out(i).wait_send())
+    steps(1, NB, lambda i: m_out(i).wait_send())
     steps(1, NB, lambda i: b_out(i).wait_send())
     steps(1, NB, lambda i: b_home(i, me).wait_send())
     steps(1, NB, lambda i: a_home(i, me).wait_send())
@@ -462,21 +507,21 @@
         out_specs=(res,) * 3,
         scratch_shapes=[
             vm((512, PW), BF16), vm((512, 256), BF16),
-            vm((512, QW + 128), BF16), vm((512, QW + 128), BF16),
+            vm((512, QW), BF16), vm((512, QW), BF16),
             vm((512, PW), BF16), vm((512, PW), BF16),
             vm((512, QW), BF16), vm((512, PW), BF16),
             vm((256, QW), BF16), vm((256, PW), BF16), vm((512, QW), BF16),
             vm((512, 512), BF16),
             vm((16, 256), I32), vm((128, 256), BF16),
             vm((1, 32), I32), vm((1, 32), I32), vm((1, 128), I32),
-            vm((256, 128), BF16),
+            vm((NB, 1, 128), F32), vm((NB, 1, 128), F32), vm((NB, 128), F32),
             vm((256, D + 128), BF16), vm((D, 256), BF16), vm((256, D), BF16),
             vm((256, 256), F32), vm((256, 256), F32), vm((256, 256), F32),
             vm((256, 256), BF16),
             vm((256, D), BF16), vm((2, 64, PW), BF16), vm((2, 64, D), BF16),
             vm((8, 256), F32), vm((3, 8, 256), F32),
         ]
-        + [dma((NB,))] * 8
+        + [dma((NB,))] * 10
         + [dma((24,))] * 2
         + [dma((3,))] * 2
         + [dma((6,))] * 2

time: 83.8 us -> 83.4 us (level)
  no operation moved by 1% of the time
where the time goes in v6:
time: 83.4 us; the launch traced here: 83.3 us
  Pallas kernels  82.6 us (99%)
    pallas_call x1, Pallas kernels, per_device(): pl.pallas_call(kernel, out_shape=(pltpu.VMEM((512, QW), BF16), pltpu.VMEM...  81.5 us

profile of v6, /device:TPU:1, one launch (start us, length us, event | category | flops | bytes accessed | tf_op | source)
XLA Modules:
  0.0 83.3 jit_solution(13435162709377297351)
XLA Ops:
  0.6 81.5 %contrastive.1 = (bf16[512,512]{1,0:T(8,128)(2,1)S(1)}, bf16[128,4096]{1,0:T(8,128)(2,1)S(1)}, bf16[512,256]{1,0:T(8,128)(2,1)S(1)}) custom-call(bf16[32,4096]{1,0:T(8,128)(2,1)} %q_hbm.1, bf16[128,4096]{1,0:T(8,128)(2,1)} %p_hbm.1, s32[1,32]{1,0:T(1,128)} %bitcast.5, s32[1,32]{1,0:T(1,128)} %bitcast.6, s32[1,128]{1,0:T(1,128)} %bitcast.7, s32[16,256]{1,0:T(8,128)} %bitcast.4), custom_call_target="tpu_custom_call" | custom-call | tf_op jit(solution)/shard_map/contrastive/pallas_call | solution.py:499
  82.1 1.1 %unpack.1 = (bf16[32,4096]{1,0:T(8,128)(2,1)}, bf16[128,4096]{1,0:T(8,128)(2,1)}) custom-call(bf16[512,512]{1,0:T(8,128)(2,1)S(1)} %get-tuple-element.5.a_back, bf16[128,4096]{1,0:T(8,128)(2,1)S(1)} %get-tuple-element.6.p_grad, bf16[512,256]{1,0:T(8,128)(2,1)S(1)} %get-tuple-element.7.g_q), custom_call_target="tpu_custom_call" | custom-call | tf_op jit(solution)/shard_map/unpack/pallas_call | solution.py:541

commit v7 on v6

--- a/solution.py
+++ b/solution.py
@@ -52,9 +52,10 @@
 
 
 def offset(i):
-    j = i % 16
+    dc = ((i + 15) // 16) % 2
+    j = (i + 15 * dc) % 16
     dx = j % 4
-    return dx, (dx + 4 - j // 4) % 4, i // 16
+    return dx, (dx + 4 - j // 4) % 4, dc
 
 
 def hops(i):
@@ -171,6 +172,14 @@
         load.wait()
     a_send[...] = nn(g_q[...], q_stack[...]).astype(BF16)
 
+    for load in loads[12:]:
+        load.wait()
+
+    def pack_p(j, carry):
+        b_send[:, cols(j)] = nn(g_p[...], p_stack[:, cols(j)]).astype(BF16)
+        return carry
+
+    lax.fori_loop(0, 2, pack_p, 0)
     pl.semaphore_wait(barrier, NB - 1 + NZ - 1)
 
     def out_copy(src, dst, send, recv, i):
@@ -237,18 +246,10 @@
         m_out(i).start()
 
     steps(1, NB, send_queries)
+    lax.fori_loop(2, PW // CT, pack_p, 0)
+    steps(1, NB, lambda i: b_out(i).start())
     a_recv[0:16, :] = a_send[mine, :]
     m_recv[0] = m_send[me]
-
-    for load in loads[12:]:
-        load.wait()
-
-    def pack_p(j, carry):
-        b_send[:, cols(j)] = nn(g_p[...], p_stack[:, cols(j)]).astype(BF16)
-        return carry
-
-    lax.fori_loop(0, PW // CT, pack_p, 0)
-    steps(1, NB, lambda i: b_out(i).start())
     b_recv[0:16, :] = b_send[mine, :]
 
     sr, sc = iota((512, 512), 0), iota((512, 512), 1)
@@ -358,8 +359,10 @@
     q_lo, q_hi = q_dig[0:1, :], q_dig[1:2, :]
     q_code = jnp.where(q_lo > 0.5, q_hi * 256.0 + q_lo, -2.0)
     slot = shr(iota((256, 1), 0), 3)
-    dx, dc = slot & 3, shr(slot, 4)
-    dy = (dx - shr(slot & 15, 2)) & 3
+    dc = shr(slot + 15, 4) & 1
+    j = (slot + 15 * dc) & 15
+    dx = j & 3
+    dy = (dx - shr(j, 2)) & 3
     p_dev = (((x - dx) & 3) * 8 + ((y - dy) & 3) * 2 + ((c + dc) & 1)) * NZ + z
     p_code = jnp.where(p_lo > 0.5, p_dev.astype(F32) * 256.0 + p_lo, -1.0)
     target[...] = jnp.where(p_code == q_code, SCALE, 0.0)

time: 83.4 us -> 82.6 us (level)
  Pallas kernels: 82.6 us -> 81.2 us
    pallas_call x1, Pallas kernels: 81.5 us -> 80 us  [per_device(): pl.pallas_call(kernel, out_shape=(pltpu.VMEM((512, QW), BF16), pltpu.VMEM...]
where the time goes in v7:
time: 82.6 us; the launch traced here: 81.8 us
  Pallas kernels  81.2 us (98%)
    pallas_call x1, Pallas kernels, per_device(): pl.pallas_call(kernel, out_shape=(pltpu.VMEM((512, QW), BF16), pltpu.VMEM...  80 us

profile of v7, /device:TPU:1, one launch (start us, length us, event | category | flops | bytes accessed | tf_op | source)
XLA Modules:
  0.0 81.8 jit_solution(9774161499052659229)
XLA Ops:
  0.6 80.0 %contrastive.1 = (bf16[512,512]{1,0:T(8,128)(2,1)S(1)}, bf16[128,4096]{1,0:T(8,128)(2,1)S(1)}, bf16[512,256]{1,0:T(8,128)(2,1)S(1)}) custom-call(bf16[32,4096]{1,0:T(8,128)(2,1)} %q_hbm.1, bf16[128,4096]{1,0:T(8,128)(2,1)} %p_hbm.1, s32[1,32]{1,0:T(1,128)} %bitcast.5, s32[1,32]{1,0:T(1,128)} %bitcast.6, s32[1,128]{1,0:T(1,128)} %bitcast.7, s32[16,256]{1,0:T(8,128)} %bitcast.4), custom_call_target="tpu_custom_call" | custom-call | tf_op jit(solution)/shard_map/contrastive/pallas_call | solution.py:502
  80.6 1.1 %unpack.1 = (bf16[32,4096]{1,0:T(8,128)(2,1)}, bf16[128,4096]{1,0:T(8,128)(2,1)}) custom-call(bf16[512,512]{1,0:T(8,128)(2,1)S(1)} %get-tuple-element.5.a_back, bf16[128,4096]{1,0:T(8,128)(2,1)S(1)} %get-tuple-element.6.p_grad, bf16[512,256]{1,0:T(8,128)(2,1)S(1)} %get-tuple-element.7.g_q), custom_call_target="tpu_custom_call" | custom-call | tf_op jit(solution)/shard_map/unpack/pallas_call | solution.py:544

commit v8 on v7

--- a/solution.py
+++ b/solution.py
@@ -439,6 +439,14 @@
         send_home(g)
     b_back[mine, :] = b_ret[0:16, :]
 
+    steps(1, NB, lambda i: a_out(i).wait_send())
+    steps(1, NB, lambda i: m_out(i).wait_send())
+    steps(1, NB, lambda i: b_out(i).wait_send())
+    for copy in q_out:
+        copy.wait_send()
+    for dz in (1, 3, 2):
+        st_out[dz].wait_send()
+
     pt_out[0].wait_recv()
     up = part[block_rows(1), low].astype(F32) + relay_in[0].astype(F32)
     part[block_rows(1), low] = up.astype(BF16)
@@ -458,23 +466,17 @@
     a_ret[...] = tn(sel_q[...], gq_stack[...]).astype(BF16)
     steps(1, NB, lambda i: a_home(i, me).start())
     a_back[mine, :] = a_ret[0:16, :]
+    for copy in pt_out:
+        copy.wait_send()
     steps(1, NB, lambda i: b_home(i, partner(i)).wait_recv())
     for j in range(PW // CT):
         got = tn(g_p[...], b_back[:, j * CT : (j + 1) * CT]).astype(BF16)
         for h in range(2):
             columns = slice(h * PW + j * CT, h * PW + (j + 1) * CT)
             p_grad[:, columns] = got[h * 128 : (h + 1) * 128, :]
-    steps(1, NB, lambda i: a_home(i, partner(i)).wait_recv())
-
-    steps(1, NB, lambda i: a_out(i).wait_send())
-    steps(1, NB, lambda i: m_out(i).wait_send())
-    steps(1, NB, lambda i: b_out(i).wait_send())
     steps(1, NB, lambda i: b_home(i, me).wait_send())
     steps(1, NB, lambda i: a_home(i, me).wait_send())
-    for copy in q_out + pt_out:
-        copy.wait_send()
-    for dz in (1, 3, 2):
-        st_out[dz].wait_send()
+    steps(1, NB, lambda i: a_home(i, partner(i)).wait_recv())
 
 
 def unpack(a_back, p_grad, g_q, outq_hbm, outp_hbm, q_buf, sem):

time: 82.6 us -> 81.5 us (0.987)
  Pallas kernels: 81.2 us -> 80.1 us
    pallas_call x1, Pallas kernels: 80 us -> 78.9 us  [per_device(): pl.pallas_call(kernel, out_shape=(pltpu.VMEM((512, QW), BF16), pltpu.VMEM...]
where the time goes in v8:
time: 81.5 us; the launch traced here: 80.7 us
  Pallas kernels  80.1 us (98%)
    pallas_call x1, Pallas kernels, per_device(): pl.pallas_call(kernel, out_shape=(pltpu.VMEM((512, QW), BF16), pltpu.VMEM...  78.9 us

profile of v8, /device:TPU:1, one launch (start us, length us, event | category | flops | bytes accessed | tf_op | source)
XLA Modules:
  0.0 80.7 jit_solution(7198841467703447028)
XLA Ops:
  0.6 78.9 %contrastive.1 = (bf16[512,512]{1,0:T(8,128)(2,1)S(1)}, bf16[128,4096]{1,0:T(8,128)(2,1)S(1)}, bf16[512,256]{1,0:T(8,128)(2,1)S(1)}) custom-call(bf16[32,4096]{1,0:T(8,128)(2,1)} %q_hbm.1, bf16[128,4096]{1,0:T(8,128)(2,1)} %p_hbm.1, s32[1,32]{1,0:T(1,128)} %bitcast.5, s32[1,32]{1,0:T(1,128)} %bitcast.6, s32[1,128]{1,0:T(1,128)} %bitcast.7, s32[16,256]{1,0:T(8,128)} %bitcast.4), custom_call_target="tpu_custom_call" | custom-call | tf_op jit(solution)/shard_map/contrastive/pallas_call | solution.py:504
  79.6 1.1 %unpack.1 = (bf16[32,4096]{1,0:T(8,128)(2,1)}, bf16[128,4096]{1,0:T(8,128)(2,1)}) custom-call(bf16[512,512]{1,0:T(8,128)(2,1)S(1)} %get-tuple-element.5.a_back, bf16[128,4096]{1,0:T(8,128)(2,1)S(1)} %get-tuple-element.6.p_grad, bf16[512,256]{1,0:T(8,128)(2,1)S(1)} %get-tuple-element.7.g_q), custom_call_target="tpu_custom_call" | custom-call | tf_op jit(solution)/shard_map/unpack/pallas_call | solution.py:546

commit v9 on v8

--- a/solution.py
+++ b/solution.py
@@ -52,10 +52,11 @@
 
 
 def offset(i):
-    dc = ((i + 15) // 16) % 2
-    j = (i + 15 * dc) % 16
-    dx = j % 4
-    return dx, (dx + 4 - j // 4) % 4, dc
+    div, rem = (int.__floordiv__, int.__mod__) if isinstance(i, int) else (lax.div, lax.rem)
+    dc = rem(div(i + 15, 16), 2)
+    j = rem(i + 15 * dc, 16)
+    dx = rem(j, 4)
+    return dx, rem(dx + 4 - div(j, 4), 4), dc
 
 
 def hops(i):
@@ -80,11 +81,11 @@
 
     def partner(i):
         dx, dy, dc = offset(i)
-        return ((x + dx) % 4) * 8 + ((y + dy) % 4) * 2 + (c + dc) % 2
+        return lax.rem(x + dx, 4) * 8 + lax.rem(y + dy, 4) * 2 + lax.rem(c + dc, 2)
 
     def origin(i):
         dx, dy, dc = offset(i)
-        return ((x + 4 - dx) % 4) * 8 + ((y + 4 - dy) % 4) * 2 + (c + dc) % 2
+        return lax.rem(x + 4 - dx, 4) * 8 + lax.rem(y + 4 - dy, 4) * 2 + lax.rem(c + dc, 2)
 
     barrier = pltpu.get_barrier_semaphore()
     for i in FAR_FIRST:

time: 81.5 us -> 81.1 us (level)
  no operation moved by 1% of the time
where the time goes in v9:
time: 81.1 us; the launch traced here: 80.6 us
  Pallas kernels  79.9 us (99%)
    pallas_call x1, Pallas kernels, per_device(): pl.pallas_call(kernel, out_shape=(pltpu.VMEM((512, QW), BF16), pltpu.VMEM...  78.8 us

profile of v9, /device:TPU:1, one launch (start us, length us, event | category | flops | bytes accessed | tf_op | source)
XLA Modules:
  0.0 80.6 jit_solution(14614313831718444278)
XLA Ops:
  0.6 78.8 %contrastive.1 = (bf16[512,512]{1,0:T(8,128)(2,1)S(1)}, bf16[128,4096]{1,0:T(8,128)(2,1)S(1)}, bf16[512,256]{1,0:T(8,128)(2,1)S(1)}) custom-call(bf16[32,4096]{1,0:T(8,128)(2,1)} %q_hbm.1, bf16[128,4096]{1,0:T(8,128)(2,1)} %p_hbm.1, s32[1,32]{1,0:T(1,128)} %bitcast.5, s32[1,32]{1,0:T(1,128)} %bitcast.6, s32[1,128]{1,0:T(1,128)} %bitcast.7, s32[16,256]{1,0:T(8,128)} %bitcast.4), custom_call_target="tpu_custom_call" | custom-call | tf_op jit(solution)/shard_map/contrastive/pallas_call | solution.py:505
  79.4 1.1 %unpack.1 = (bf16[32,4096]{1,0:T(8,128)(2,1)}, bf16[128,4096]{1,0:T(8,128)(2,1)}) custom-call(bf16[512,512]{1,0:T(8,128)(2,1)S(1)} %get-tuple-element.5.a_back, bf16[128,4096]{1,0:T(8,128)(2,1)S(1)} %get-tuple-element.6.p_grad, bf16[512,256]{1,0:T(8,128)(2,1)S(1)} %get-tuple-element.7.g_q), custom_call_target="tpu_custom_call" | custom-call | tf_op jit(solution)/shard_map/unpack/pallas_call | solution.py:547
